TPU v7x, 32 devices: a whole 2x2x4 slice. The times are simulated.
32 devices in a mesh: groups: 2 (over y), tile: 4 (over z), pos: 4 (over x, core).
Axes of the slice: x: 2, y: 2, z: 4, core: 2. Of those that a mesh axis runs over, the one named last changes fastest.
Arguments:
- object_field: float32 [4, 2, 256, 1024], P('groups', None, 'tile'), parts along dimension 0, may hold values from -8 to 8
- probe_modes: float32 [8, 2, 128, 128], P('groups'), parts along dimension 0, may hold values from -6 to 6
- measured: float32 [8, 4, 8, 128, 128], P(('groups', 'tile'), 'pos'), parts along dimension 0, may hold values from 0.2 to 2
- row_offset: int32 [8, 4, 8], P(('groups', 'tile'), 'pos'), parts along dimension 0, may hold values from 0 to 63
- col_offset: int32 [8, 4, 8], P(('groups', 'tile'), 'pos'), parts along dimension 0, may hold values from 0 to 896
- position_count: int32 [8, 4], P(('groups', 'tile'), 'pos'), parts along dimension 0, may hold values from 1 to 8, as said below
Outputs:
- object_update: float32 [4, 2, 256, 1024], P('groups', None, 'tile'), parts along dimension 0
- probe_update: float32 [8, 2, 128, 128], P('groups'), parts along dimension 0
There are 2 independent parts, one for each index of `groups`. A program takes and returns all parts, laid end to end along the dimension named above; each array names one. Nothing has to cross between parts.
Inputs may be any that keep to these rules, and one draw needn't show every extreme that they name: `position_count`: every device has at least one live slot and some device has 8.
All inputs are finite; a program needn't handle non-finite values.
Results may differ from a plain program's by a relative error of at most 0.0001.
Values sent between devices are 32-bit elements; how exact they have to be, the bound alone decides.
A program may use at most 64 MiB of HBM per device.

v0:
```python
import math

import jax
import jax.numpy as jnp
from jax import lax
from jax.sharding import PartitionSpec as P

PATCH = 128


FRESNEL = 0.25
RELAX = 1.0
PROBE_RATE = 4.0


def passed_along(value, axis, by):
    devices = lax.axis_size(axis)
    pairs = [(i, i + by) for i in range(devices) if 0 <= i + by < devices]
    return lax.ppermute(value, axis, pairs)


def product_high(left_mat, right_mat):
    return jnp.dot(
        left_mat, right_mat, precision=lax.Precision.HIGHEST, preferred_element_type=jnp.float32
    )


def complex_tables():
    indices = jnp.arange(PATCH, dtype=jnp.int32)
    products = indices[:, None] * indices[None, :] % PATCH
    angle_tab = 2.0 * math.pi / PATCH * products.astype(jnp.float32)
    scale_tab = 1.0 / math.sqrt(PATCH)
    fourier_re = jnp.cos(angle_tab) * scale_tab
    fourier_im = -jnp.sin(angle_tab) * scale_tab
    frequency = (
        jnp.where(indices < PATCH // 2, indices, indices - PATCH).astype(jnp.float32) / PATCH
    )
    phase_tab = -math.pi * FRESNEL * PATCH * frequency * frequency
    kernel_re = jnp.cos(phase_tab)
    kernel_im = jnp.sin(phase_tab)
    left_re = fourier_re * kernel_re[None, :] + fourier_im * kernel_im[None, :]
    left_im = fourier_re * kernel_im[None, :] - fourier_im * kernel_re[None, :]
    propagator_re = product_high(left_re, fourier_re) - product_high(left_im, fourier_im)
    propagator_im = product_high(left_re, fourier_im) + product_high(left_im, fourier_re)
    return (fourier_re, fourier_im, propagator_re, propagator_im)


def apply_both(mat_re, mat_im, field_re, field_im):
    highest = lax.Precision.HIGHEST
    half_re = jnp.einsum("ij,mjk->mik", mat_re, field_re, precision=highest) - jnp.einsum(
        "ij,mjk->mik", mat_im, field_im, precision=highest
    )
    half_im = jnp.einsum("ij,mjk->mik", mat_re, field_im, precision=highest) + jnp.einsum(
        "ij,mjk->mik", mat_im, field_re, precision=highest
    )
    done_re = jnp.einsum("mij,kj->mik", half_re, mat_re, precision=highest) - jnp.einsum(
        "mij,kj->mik", half_im, mat_im, precision=highest
    )
    done_im = jnp.einsum("mij,kj->mik", half_re, mat_im, precision=highest) + jnp.einsum(
        "mij,kj->mik", half_im, mat_re, precision=highest
    )
    return (done_re, done_im)


def slot_loss(patches, probe_modes, measured_one, tables):
    fourier_re, fourier_im, propagator_re, propagator_im = tables
    wave_re = probe_modes[:, 0] * patches[0, 0] - probe_modes[:, 1] * patches[0, 1]
    wave_im = probe_modes[:, 0] * patches[0, 1] + probe_modes[:, 1] * patches[0, 0]
    wave_re, wave_im = apply_both(propagator_re, propagator_im, wave_re, wave_im)
    next_re = wave_re * patches[1, 0] - wave_im * patches[1, 1]
    wave_im = wave_re * patches[1, 1] + wave_im * patches[1, 0]
    detector_re, detector_im = apply_both(fourier_re, fourier_im, next_re, wave_im)
    intensity = jnp.sum(detector_re * detector_re + detector_im * detector_im, axis=0)
    misfit = intensity - measured_one
    return 0.5 * jnp.sum(misfit * misfit)


def per_device(object_field, probe_modes, measured, row_offset, col_offset, position_count):
    tables = complex_tables()
    gradient = jax.grad(slot_loss, argnums=(0, 1))
    layers = object_field.shape[0]
    strip_rows = object_field.shape[2]
    width_cols = object_field.shape[3]
    patch_side = probe_modes.shape[2]
    reach_strips = patch_side // strip_rows
    below_list = [
        passed_along(object_field, "tile", -shift_by) for shift_by in range(1, reach_strips + 1)
    ]
    extended = jnp.concatenate([object_field] + below_list, axis=2)
    ext_rows = extended.shape[2]
    lighting = jnp.sum(
        probe_modes[:, 0] * probe_modes[:, 0] + probe_modes[:, 1] * probe_modes[:, 1], axis=0
    )
    initial = (
        jnp.zeros((2 * layers + 1, ext_rows, width_cols), jnp.float32),
        jnp.zeros_like(probe_modes),
        jnp.zeros((patch_side, patch_side), jnp.float32),
    )

    def accumulate(running, top_row, left_col, measured_one):
        stacked, probe_sum, norm_sum = running
        zero_index = jnp.zeros((), jnp.int32)
        patches = lax.dynamic_slice(
            extended,
            (zero_index, zero_index, top_row, left_col),
            (layers, 2, patch_side, patch_side),
        )
        patch_grad, probe_grad = gradient(patches, probe_modes, measured_one, tables)
        term = jnp.concatenate(
            [patch_grad.reshape(2 * layers, patch_side, patch_side), lighting[None]], axis=0
        )
        current = lax.dynamic_slice(
            stacked, (zero_index, top_row, left_col), (2 * layers + 1, patch_side, patch_side)
        )
        stacked = lax.dynamic_update_slice(stacked, current + term, (zero_index, top_row, left_col))
        probe_sum = probe_sum + probe_grad
        norm_sum = norm_sum + (patches[0, 0] * patches[0, 0] + patches[0, 1] * patches[0, 1])
        return (stacked, probe_sum, norm_sum)

    measured_here = measured.reshape(-1, patch_side, patch_side)
    rows_here = row_offset.reshape(-1)
    cols_here = col_offset.reshape(-1)
    live_count = position_count.reshape(())

    def visit_own(slot_id, running):
        return accumulate(running, rows_here[slot_id], cols_here[slot_id], measured_here[slot_id])

    totals = lax.fori_loop(0, live_count, visit_own, initial)
    stacked, probe_sum, norm_sum = totals
    upper_rows = stacked[:, :strip_rows]
    for shift_by in range(1, reach_strips + 1):
        rim_rows = stacked[:, shift_by * strip_rows : (shift_by + 1) * strip_rows]
        upper_rows = upper_rows + passed_along(rim_rows, "tile", shift_by)
    summed = lax.psum(upper_rows, "pos")
    update_flat = -summed[: 2 * layers] / (summed[2 * layers][None] + RELAX)
    object_update = update_flat.reshape(layers, 2, strip_rows, width_cols)
    probe_total, norm_total = lax.psum((probe_sum, norm_sum), ("tile", "pos"))
    probe_update = -PROBE_RATE * probe_total / (norm_total[None, None] + RELAX)
    return (object_update, probe_update)


def solution(mesh):
    return jax.shard_map(
        per_device,
        mesh=mesh,
        in_specs=(
            P("groups", None, "tile", None),
            P("groups", None, None, None),
            P(("groups", "tile"), "pos", None, None, None),
            P(("groups", "tile"), "pos", None),
            P(("groups", "tile"), "pos", None),
            P(("groups", "tile"), "pos"),
        ),
        out_specs=(P("groups", None, "tile", None), P("groups", None, None, None)),
        check_vma=False,
    )
```

profile of v0, /device:TPU:23, one launch (start us, length us, event | category | flops | bytes accessed | tf_op | source)
XLA Modules:
  0.0 552.9 jit_solution(4776621263658921167)
XLA Ops:
  7.2 2.2 collective-permute-start
  9.4 2.3 collective-permute-start.1
  11.8 1.2 copy.95
  16.0 17.4 %collective-permute-done = f32[2,2,64,1024]{3,2,1,0:T(8,128)S(1)} collective-permute-done((f32[2,2,64,1024]{3,2,1,0:T(8,128)}, f32[2,2,64,1024]{3,2,1,0:T(8,128)S(1)}, u32[]{:S(2)}, u32[]{:S(2)}) %collective-permute-start) | collective-permute-done | bytes 1048608 | tf_op jit(solution)/shard_map/ppermute | solution.py:19
  33.5 43.0 %collective-permute-done.1 = f32[2,2,64,1024]{3,2,1,0:T(8,128)} collective-permute-done((f32[2,2,64,1024]{3,2,1,0:T(8,128)}, f32[2,2,64,1024]{3,2,1,0:T(8,128)}, u32[]{:S(2)}, u32[]{:S(2)}) %collective-permute-start.1) | collective-permute-done | bytes 1048608 | tf_op jit(solution)/shard_map/ppermute | solution.py:19
  76.5 3.2 pad_maximum_fusion
  79.8 2.4 broadcast_in_dim.59
  82.2 294.5 %while.16 = (s32[]{:T(128)}, f32[5,192,1024]{2,1,0:T(8,128)}, f32[4,2,128,128]{2,3,0,1:T(8,128)S(1)}, f32[128,128]{1,0:T(8,128)S(1)}, s32[]{:T(128)}, /*index=5*...) while((s32[]{:T(128)}, f32[5,192,1024]{2,1,0:T(8,128)}, ...), condition=%wide.region_11.12_spmd.clone.clone, body=%wide.region_1.11_spmd.clone.clone.sunk | while | flops 3232432128 | bytes 36503908 | solution.py:128
  88.1 1.1 dynamic-slice_bitcast_fusion.7
  89.2 1.1 add_add_fusion.5
  110.8 1.3 maximum_add_fusion.2
  112.3 6.9 %dynamic_update_slice.6 = f32[5,192,1024]{2,1,0:T(8,128)} dynamic-update-slice(f32[5,192,1024]{2,1,0:T(8,128)} %get-tuple-element.444, f32[5,128,128]{2,1,0:T(8,128)S(1)} %maximum_add_fusion.2, s32[]{:T(128)} %constant.26.clone.1..sunk, s32[]{:T(128)S(6)} %select_n.246, s32[]{:T(128)S(6)} %select_n.247) | dynamic-update-slice | bytes 655364 | tf_op jit(solution)/shard_map/while/body/dynamic_update_slice | solution.py:115
  124.9 1.1 dynamic-slice_bitcast_fusion.7
  126.0 1.1 add_add_fusion.5
  147.7 1.3 maximum_add_fusion.2
  149.1 6.8 %dynamic_update_slice.6 = f32[5,192,1024]{2,1,0:T(8,128)} dynamic-update-slice(f32[5,192,1024]{2,1,0:T(8,128)} %get-tuple-element.444, f32[5,128,128]{2,1,0:T(8,128)S(1)} %maximum_add_fusion.2, s32[]{:T(128)} %constant.26.clone.1..sunk, s32[]{:T(128)S(6)} %select_n.246, s32[]{:T(128)S(6)} %select_n.247) | dynamic-update-slice | bytes 655364 | tf_op jit(solution)/shard_map/while/body/dynamic_update_slice | solution.py:115
  161.7 1.1 dynamic-slice_bitcast_fusion.7
  162.7 1.1 add_add_fusion.5
  184.4 1.3 maximum_add_fusion.2
  185.9 6.6 %dynamic_update_slice.6 = f32[5,192,1024]{2,1,0:T(8,128)} dynamic-update-slice(f32[5,192,1024]{2,1,0:T(8,128)} %get-tuple-element.444, f32[5,128,128]{2,1,0:T(8,128)S(1)} %maximum_add_fusion.2, s32[]{:T(128)} %constant.26.clone.1..sunk, s32[]{:T(128)S(6)} %select_n.246, s32[]{:T(128)S(6)} %select_n.247) | dynamic-update-slice | bytes 655364 | tf_op jit(solution)/shard_map/while/body/dynamic_update_slice | solution.py:115
  198.2 1.1 dynamic-slice_bitcast_fusion.7
  199.3 1.1 add_add_fusion.5
  220.9 1.3 maximum_add_fusion.2
  222.4 6.7 %dynamic_update_slice.6 = f32[5,192,1024]{2,1,0:T(8,128)} dynamic-update-slice(f32[5,192,1024]{2,1,0:T(8,128)} %get-tuple-element.444, f32[5,128,128]{2,1,0:T(8,128)S(1)} %maximum_add_fusion.2, s32[]{:T(128)} %constant.26.clone.1..sunk, s32[]{:T(128)S(6)} %select_n.246, s32[]{:T(128)S(6)} %select_n.247) | dynamic-update-slice | bytes 655364 | tf_op jit(solution)/shard_map/while/body/dynamic_update_slice | solution.py:115
  234.9 1.1 dynamic-slice_bitcast_fusion.7
  236.0 1.1 add_add_fusion.5
  257.6 1.3 maximum_add_fusion.2
  259.1 6.9 %dynamic_update_slice.6 = f32[5,192,1024]{2,1,0:T(8,128)} dynamic-update-slice(f32[5,192,1024]{2,1,0:T(8,128)} %get-tuple-element.444, f32[5,128,128]{2,1,0:T(8,128)S(1)} %maximum_add_fusion.2, s32[]{:T(128)} %constant.26.clone.1..sunk, s32[]{:T(128)S(6)} %select_n.246, s32[]{:T(128)S(6)} %select_n.247) | dynamic-update-slice | bytes 655364 | tf_op jit(solution)/shard_map/while/body/dynamic_update_slice | solution.py:115
  271.7 1.1 dynamic-slice_bitcast_fusion.7
  272.8 1.1 add_add_fusion.5
  294.5 1.3 maximum_add_fusion.2
  295.9 6.7 %dynamic_update_slice.6 = f32[5,192,1024]{2,1,0:T(8,128)} dynamic-update-slice(f32[5,192,1024]{2,1,0:T(8,128)} %get-tuple-element.444, f32[5,128,128]{2,1,0:T(8,128)S(1)} %maximum_add_fusion.2, s32[]{:T(128)} %constant.26.clone.1..sunk, s32[]{:T(128)S(6)} %select_n.246, s32[]{:T(128)S(6)} %select_n.247) | dynamic-update-slice | bytes 655364 | tf_op jit(solution)/shard_map/while/body/dynamic_update_slice | solution.py:115
  309.5 1.1 add_add_fusion.5
  331.1 1.3 maximum_add_fusion.2
  332.6 6.7 %dynamic_update_slice.6 = f32[5,192,1024]{2,1,0:T(8,128)} dynamic-update-slice(f32[5,192,1024]{2,1,0:T(8,128)} %get-tuple-element.444, f32[5,128,128]{2,1,0:T(8,128)S(1)} %maximum_add_fusion.2, s32[]{:T(128)} %constant.26.clone.1..sunk, s32[]{:T(128)S(6)} %select_n.246, s32[]{:T(128)S(6)} %select_n.247) | dynamic-update-slice | bytes 655364 | tf_op jit(solution)/shard_map/while/body/dynamic_update_slice | solution.py:115
  345.0 1.1 dynamic-slice_bitcast_fusion.7
  346.1 1.1 add_add_fusion.5
  367.8 1.3 maximum_add_fusion.2
  369.2 6.6 %dynamic_update_slice.6 = f32[5,192,1024]{2,1,0:T(8,128)} dynamic-update-slice(f32[5,192,1024]{2,1,0:T(8,128)} %get-tuple-element.444, f32[5,128,128]{2,1,0:T(8,128)S(1)} %maximum_add_fusion.2, s32[]{:T(128)} %constant.26.clone.1..sunk, s32[]{:T(128)S(6)} %select_n.246, s32[]{:T(128)S(6)} %select_n.247) | dynamic-update-slice | bytes 655364 | tf_op jit(solution)/shard_map/while/body/dynamic_update_slice | solution.py:115
  376.7 3.6 fusion.226
  380.3 1.9 collective-permute-start.2
  382.2 1.3 collective-permute-start.3
  384.5 42.7 %collective-permute-done.2 = f32[5,64,1024]{2,1,0:T(8,128)S(1)} collective-permute-done((f32[5,64,1024]{2,1,0:T(8,128)}, f32[5,64,1024]{2,1,0:T(8,128)S(1)}, u32[]{:S(2)}, u32[]{:S(2)}) %collective-permute-start.2) | collective-permute-done | bytes 1310752 | tf_op jit(solution)/shard_map/ppermute | solution.py:19
  427.2 3.2 add_add_fusion.2
  430.4 69.4 %all-reduce.18.cloned.1.call-done = (f32[4,2,128,128]{3,2,1,0:T(8,128)}, f32[128,128]{1,0:T(8,128)}) async-done(((f32[4,2,128,128]{3,2,1,0:T(8,128)}, f32[128,128]{1,0:T(8,128)}), (f32[4,2,128,128]{3,2,1,0:T(8,128)}, f32[128,128]{1,0:T(8,128)})) %all-reduce.18.cloned.1.call-update) | async-done | bytes 589840 | tf_op jit(solution)/shard_map/psum | solution.py:137
  500.7 1.9 multiply_divide_fusion
  502.6 40.2 %all-reduce.16.cloned.1.call-done = f32[5,64,1024]{2,1,0:T(8,128)} async-done(((f32[5,64,1024]{2,1,0:T(8,128)}), f32[5,64,1024]{2,1,0:T(8,128)}) %all-reduce.16.cloned.1.call-update) | async-done | bytes 1310736 | tf_op jit(solution)/shard_map/psum | solution.py:134
  543.7 2.4 fusion.170
  (369 shorter events, 179.8 us)
Async XLA Ops:
  7.2 69.3 %copy-start.1 = (f32[2,2,64,1024]{3,2,1,0:T(8,128)S(1)}, f32[2,2,64,1024]{3,2,1,0:T(8,128)}, u32[]{:S(2)}) copy-start(f32[2,2,64,1024]{3,2,1,0:T(8,128)} %param.8) | copy-start | bytes 3145732
  7.2 492.7 %all-reduce.18.cloned.1.call-start = ((), (), s32[]{:S(2)}) async-start(), calls=%async_computation.1 | async-start | bytes 1179648 | tf_op jit(solution)/shard_map/psum | solution.py:137
  7.2 26.3 %collective-permute-start = (f32[2,2,64,1024]{3,2,1,0:T(8,128)}, f32[2,2,64,1024]{3,2,1,0:T(8,128)S(1)}, u32[]{:S(2)}, u32[]{:S(2)}) collective-permute-start(f32[2,2,64,1024]{3,2,1,0:T(8,128)} %param.8), channel_id=1, source_target_pairs={{4,0},{8,4},{12,8},{5,1},{9,5},{13,9},{6,2},{10,6},{14,10},{7,3},{... | collective-permute-start | bytes 3145736 | tf_op jit(solution)/shard_map/ppermute | solution.py:19
  9.4 67.1 %collective-permute-start.1 = (f32[2,2,64,1024]{3,2,1,0:T(8,128)}, f32[2,2,64,1024]{3,2,1,0:T(8,128)}, u32[]{:S(2)}, u32[]{:S(2)}) collective-permute-start(f32[2,2,64,1024]{3,2,1,0:T(8,128)} %param.8), channel_id=1, source_target_pairs={{8,0},{12,4},{9,1},{13,5},{10,2},{14,6},{11,3},{15,7},{24,16},{28,... | collective-permute-start | bytes 3145736 | tf_op jit(solution)/shard_map/ppermute | solution.py:19
  79.7 2.4 copy-start.2
  79.7 2.4 copy-start.3
  376.7 7.8 %copy-start = (f32[128,128]{1,0:T(8,128)}, f32[128,128]{1,0:T(8,128)S(1)}, u32[]{:S(2)}) copy-start(f32[128,128]{1,0:T(8,128)S(1)} %get-tuple-element.126) | copy-start | bytes 196612
  380.3 47.0 %collective-permute-start.2 = (f32[5,64,1024]{2,1,0:T(8,128)}, f32[5,64,1024]{2,1,0:T(8,128)S(1)}, u32[]{:S(2)}, u32[]{:S(2)}) collective-permute-start(f32[5,64,1024]{2,1,0:T(8,128)} %get-tuple-element.300), channel_id=1, source_target_pairs={{0,4},{4,8},{8,12},{1,5},{5,9},{9,13},{2,6},{6,10},{10,14},{3,7},{... | collective-permute-start | bytes 3932168 | tf_op jit(solution)/shard_map/ppermute | solution.py:19
  382.2 45.0 %collective-permute-start.3 = (f32[5,64,1024]{2,1,0:T(8,128)}, f32[5,64,1024]{2,1,0:T(8,128)}, u32[]{:S(2)}, u32[]{:S(2)}) collective-permute-start(f32[5,64,1024]{2,1,0:T(8,128)} %get-tuple-element.301), channel_id=1, source_target_pairs={{0,8},{4,12},{1,9},{5,13},{2,10},{6,14},{3,11},{7,15},{16,24},{20,... | collective-permute-start | bytes 3932168 | tf_op jit(solution)/shard_map/ppermute | solution.py:19
  384.5 158.3 %all-reduce.16.cloned.1.call-start = ((), (), s32[]{:S(2)}) async-start(), calls=%async_computation | async-start | bytes 2621440 | tf_op jit(solution)/shard_map/psum | solution.py:134
Sparse Core Ops, SparseCore 0:
  384.6 115.1 all-reduce.17
  502.2 40.4 all-reduce.15
where the time goes:
time: 550 us; the launch traced here: 553 us
  waiting for transfers between devices  213 us (39%)
  matrix products  152 us (28%)
  local copies, waits for them, and re-layouts  84.6 us (15%)
  other arithmetic  41.2 us (7%)
  loops' own time  40.1 us (7%)
  between operations  14.2 us (3%)
  starting transfers between devices  7.78 us (1%)
    ppermute x4, waiting for transfers between devices, passed_along(): return lax.ppermute(value, axis, pairs)  103 us
    psum x1, waiting for transfers between devices, per_device(): probe_total, norm_total = lax.psum((probe_sum, norm_sum), ('tile', 'pos'))  69.4 us
    dynamic_update_slice x8, local copies, waits for them, and re-layouts, accumulate(): lax.dynamic_update_slice(stacked, current + term, (zero_index, top_row, l...  53.8 us
    psum x1, waiting for transfers between devices, per_device(): summed = lax.psum(upper_rows, 'pos')  40.2 us
    another operation x1, loops' own time, per_device(): totals = lax.fori_loop(0, live_count, visit_own, initial)  40.1 us
    dot_general x32, matrix products, apply_both(): jnp.einsum('ij,mjk->mik', mat_im, field_im, precision=highest)  19.5 us
    dot_general x32, matrix products, apply_both(): jnp.einsum('ij,mjk->mik', mat_re, field_im, precision=highest)  19.2 us
    dot_general x32, matrix products, apply_both(): jnp.einsum('ij,mjk->mik', mat_re, field_re, precision=highest)  19.1 us
  transfers between devices with their start and end apart: 6, of which 5 were waited for; matrix products, arithmetic and copies ran while one was open for 2% of the time, Pallas kernels for 0%

commit v1 on v0

v1 whole, which is shorter than its diff:
```python
import functools
import math

import jax
import jax.numpy as jnp
import numpy as np
from jax import lax
from jax.experimental import pallas as pl
from jax.experimental.pallas import tpu as pltpu
from jax.sharding import PartitionSpec as P

FRESNEL = 0.25
RELAX = 1.0
PROBE_RATE = 4.0
MIB = 1024 * 1024


def passed_along(value, axis, by):
    devices = lax.axis_size(axis)
    pairs = [(i, i + by) for i in range(devices) if 0 <= i + by < devices]
    return lax.ppermute(value, axis, pairs)


def block_tables(side):
    indices = np.arange(side)
    angle = 2.0 * np.pi / side * (indices[:, None] * indices[None, :] % side)
    fourier = np.exp(-1j * angle) / np.sqrt(side)
    frequency = np.where(indices < side // 2, indices, indices - side) / side
    kernel = np.exp(-1j * math.pi * FRESNEL * side * frequency * frequency)
    propagator = (np.conj(fourier) * kernel[None, :]) @ fourier
    blocks = []
    for table in (propagator, np.conj(propagator), fourier, np.conj(fourier)):
        blocks.append(np.block([[table.real, table.imag], [-table.imag, table.real]]))
    stacked = np.stack(blocks).astype(np.float32)
    high = stacked.astype(jnp.bfloat16)
    low = (stacked - high.astype(np.float32)).astype(jnp.bfloat16)
    return high, low


def halves(value):
    high = value.astype(jnp.bfloat16)
    low = (value - high.astype(jnp.float32)).astype(jnp.bfloat16)
    return high, low


def dot(left, right):
    return jnp.dot(left, right, preferred_element_type=jnp.float32)


def both_sides(fields, right_high, right_low, left_high, left_low):
    side = fields[0][0].shape[0]
    rows = jnp.concatenate([jnp.concatenate(field, axis=1) for field in fields], axis=0)
    high, low = halves(rows)
    half = dot(high, right_high) + dot(high, right_low) + dot(low, right_high)
    tops = [half[i * side : (i + 1) * side, :side] for i in range(len(fields))]
    ends = [half[i * side : (i + 1) * side, side:] for i in range(len(fields))]
    cols = jnp.concatenate([jnp.concatenate(tops, axis=1), jnp.concatenate(ends, axis=1)], axis=0)
    high, low = halves(cols)
    done = dot(left_high, high) + dot(left_low, high) + dot(left_high, low)
    return [
        (done[:side, i * side : (i + 1) * side], done[side:, i * side : (i + 1) * side])
        for i in range(len(fields))
    ]


def times(left, right):
    return (left[0] * right[0] - left[1] * right[1], left[0] * right[1] + left[1] * right[0])


def times_conj(left, right):
    return (left[0] * right[0] + left[1] * right[1], left[1] * right[0] - left[0] * right[1])


def slots_kernel(
    row_ref, col_ref, count_ref, object_ref, probe_ref, measured_ref, high_ref, low_ref,
    stacked_ref, probe_sum_ref, norm_ref, light_ref, mid_ref, far_ref,
):
    modes, _, side, _ = probe_ref.shape
    width = object_ref.shape[2]
    stacked_ref[...] = jnp.zeros_like(stacked_ref)
    probe_sum_ref[...] = jnp.zeros_like(probe_sum_ref)
    norm_ref[...] = jnp.zeros_like(norm_ref)
    light = jnp.zeros((side, side), jnp.float32)
    for m in range(modes):
        light = light + probe_ref[m, 0] * probe_ref[m, 0] + probe_ref[m, 1] * probe_ref[m, 1]
    light_ref[...] = light
    groups = [list(range(m, min(m + 2, modes))) for m in range(0, modes, 2)]
    prop, prop_c, four, four_c = range(4)

    def apply(fields, table, conj_table):
        return both_sides(
            fields, high_ref[table], low_ref[table], high_ref[conj_table], low_ref[conj_table]
        )

    def visit(slot, carry):
        row = row_ref[slot]
        col = col_ref[slot]
        base = pl.multiple_of(jnp.minimum(col // 128 * 128, width - 2 * 128), 128)
        offset = col - base
        lane = lax.broadcasted_iota(jnp.int32, (side + 8, 128), 1)
        back = lax.rem(128 - lax.rem(offset, 128), 128)
        ahead = lax.rem(offset, 128)

        start = pl.multiple_of(row // 8 * 8, 8)
        shift = row - start
        tall = side + 8
        rise = lax.rem(tall - shift, tall)

        def patch(plane):
            first = object_ref[plane, pl.ds(start, tall), pl.ds(base, 128)]
            second = object_ref[plane, pl.ds(start, tall), pl.ds(base + 128, 128)]
            chosen = pltpu.roll(jnp.where(lane >= offset, first, second), back, 1)
            return pltpu.roll(chosen, rise, 0)[:side]

        def place(plane, value):
            value = jnp.concatenate([value, jnp.zeros((8, side), jnp.float32)], axis=0)
            value = pltpu.roll(pltpu.roll(value, ahead, 1), shift, 0)
            kept = lane >= offset
            first = jnp.where(kept, value, 0.0)
            second = jnp.where(kept, 0.0, value)
            at = (plane, pl.ds(start, tall), pl.ds(base, 128))
            stacked_ref[at] = stacked_ref[at] + first
            at = (plane, pl.ds(start, tall), pl.ds(base + 128, 128))
            stacked_ref[at] = stacked_ref[at] + second

        upper = (patch(0), patch(1))
        lower = (patch(2), patch(3))
        norm_ref[...] += upper[0] * upper[0] + upper[1] * upper[1]
        place(4, light_ref[...])
        intensity = jnp.zeros((side, side), jnp.float32)
        for group in groups:
            waves = [times((probe_ref[m, 0], probe_ref[m, 1]), upper) for m in group]
            waves = apply(waves, prop, prop_c)
            for m, wave in zip(group, waves):
                mid_ref[m, 0] = wave[0]
                mid_ref[m, 1] = wave[1]
            waves = apply([times(wave, lower) for wave in waves], four, four_c)
            for m, wave in zip(group, waves):
                far_ref[m, 0] = wave[0]
                far_ref[m, 1] = wave[1]
                intensity = intensity + wave[0] * wave[0] + wave[1] * wave[1]
        misfit = 2.0 * (intensity - measured_ref[slot])
        zero = jnp.zeros((side, side), jnp.float32)
        lower_grad = (zero, zero)
        upper_grad = (zero, zero)
        for group in groups:
            grads = [(misfit * far_ref[m, 0], misfit * far_ref[m, 1]) for m in group]
            grads = apply(grads, four_c, four)
            for m, grad in zip(group, grads):
                term = times_conj(grad, (mid_ref[m, 0], mid_ref[m, 1]))
                lower_grad = (lower_grad[0] + term[0], lower_grad[1] + term[1])
            grads = apply([times_conj(grad, lower) for grad in grads], prop_c, prop)
            for m, grad in zip(group, grads):
                term = times_conj(grad, (probe_ref[m, 0], probe_ref[m, 1]))
                upper_grad = (upper_grad[0] + term[0], upper_grad[1] + term[1])
                term = times_conj(grad, upper)
                probe_sum_ref[m, 0] += term[0]
                probe_sum_ref[m, 1] += term[1]
        place(0, upper_grad[0])
        place(1, upper_grad[1])
        place(2, lower_grad[0])
        place(3, lower_grad[1])
        return carry

    lax.fori_loop(0, count_ref[0], visit, 0)


def slots(rows, cols, count, extended, probe_modes, measured):
    modes, _, side, _ = probe_modes.shape
    high, low = block_tables(side)
    planes, ext_rows, width = extended.shape
    vmem = pl.BlockSpec(memory_space=pltpu.VMEM)
    smem = pl.BlockSpec(memory_space=pltpu.SMEM)
    return pl.pallas_call(
        slots_kernel,
        out_shape=(
            jax.ShapeDtypeStruct((planes + 1, ext_rows, width), jnp.float32),
            jax.ShapeDtypeStruct(probe_modes.shape, jnp.float32),
            jax.ShapeDtypeStruct((side, side), jnp.float32),
        ),
        in_specs=[smem] * 3 + [vmem] * 5,
        out_specs=(vmem,) * 3,
        scratch_shapes=[
            pltpu.VMEM((side, side), jnp.float32),
            pltpu.VMEM(probe_modes.shape, jnp.float32),
            pltpu.VMEM(probe_modes.shape, jnp.float32),
        ],
        compiler_params=pltpu.CompilerParams(vmem_limit_bytes=40 * MIB),
        name="slots",
    )(rows, cols, count, extended, probe_modes, measured, jnp.asarray(high), jnp.asarray(low))


def per_device(object_field, probe_modes, measured, row_offset, col_offset, position_count):
    layers, _, strip_rows, width = object_field.shape
    side = probe_modes.shape[2]
    reach = side // strip_rows
    own = object_field.reshape(2 * layers, strip_rows, width)
    below = [passed_along(own, "tile", -by) for by in range(1, reach + 1)]
    extended = jnp.concatenate([own] + below, axis=1)
    stacked, probe_sum, norm_sum = slots(
        row_offset.reshape(-1),
        col_offset.reshape(-1),
        position_count.reshape(-1),
        extended,
        probe_modes,
        measured.reshape(-1, side, side),
    )
    upper_rows = stacked[:, :strip_rows]
    for by in range(1, reach + 1):
        rim_rows = stacked[:, by * strip_rows : (by + 1) * strip_rows]
        upper_rows = upper_rows + passed_along(rim_rows, "tile", by)
    summed = lax.psum(upper_rows, "pos")
    update_flat = -summed[: 2 * layers] / (summed[2 * layers][None] + RELAX)
    object_update = update_flat.reshape(layers, 2, strip_rows, width)
    probe_total, norm_total = lax.psum((probe_sum, norm_sum), ("tile", "pos"))
    probe_update = -PROBE_RATE * probe_total / (norm_total[None, None] + RELAX)
    return (object_update, probe_update)


def solution(mesh):
    return jax.shard_map(
        per_device,
        mesh=mesh,
        in_specs=(
            P("groups", None, "tile", None),
            P("groups", None, None, None),
            P(("groups", "tile"), "pos", None, None, None),
            P(("groups", "tile"), "pos", None),
            P(("groups", "tile"), "pos", None),
            P(("groups", "tile"), "pos"),
        ),
        out_specs=(P("groups", None, "tile", None), P("groups", None, None, None)),
        check_vma=False,
    )
```

time: 550 us -> 300 us (0.55); the launches traced: 553 us -> 296 us
  matrix products: 152 us -> 0 us
  local copies, waits for them, and re-layouts: 84.6 us -> 2.27 us
  loops' own time: 40.1 us -> 0 us
  Pallas kernels: 0 us -> 39.3 us
  other arithmetic: 41.2 us -> 10.7 us
  waiting for transfers between devices: 213 us -> 222 us
    dot_general x260 -> x0, matrix products: 152 us -> none  [the longest x32 19.5 us: apply_both(): jnp.einsum('ij,mjk->mik', mat_im, field_im, precision=highest)]
    dynamic_update_slice x8 -> x0, local copies, waits for them, and re-layouts: 53.8 us -> none  [accumulate(): lax.dynamic_update_slice(stacked, current + term, (zero_index, top_row, l...]
    another operation x1 -> x0, loops' own time: 40.1 us -> none  [per_device(): totals = lax.fori_loop(0, live_count, visit_own, initial)]
    pallas_call x0 -> x1, Pallas kernels: none -> 39.3 us  [slots(): pl.pallas_call(slots_kernel, out_shape=(jax.ShapeDtypeStruct((planes + 1,...]
    add x25 -> x1, other arithmetic: 23.6 us -> 3.18 us  [per_device(): upper_rows = upper_rows + passed_along(rim_rows, 'tile', by)]
    mul x24 -> x0, local copies, waits for them, and re-layouts: 10.2 us -> none  [the longest x8 8.7 us: slot_loss(): next_re = wave_re * patches[1, 0] - wave_im * patches[1, 1]]
    dynamic_slice x16 -> x0, local copies, waits for them, and re-layouts: 9.4 us -> none  [the longest x8 4.71 us: visit_own(): cols_here[slot_id]]
    add_any x16 -> x0, other arithmetic: 7.15 us -> none  [the longest x8 6.9 us: slot_loss(): return 0.5 * jnp.sum(misfit * misfit)]
where the time goes in v1:
time: 300 us; the launch traced here: 296 us
  waiting for transfers between devices  222 us (74%)
  Pallas kernels  39.3 us (13%)
  between operations  14.8 us (5%)
  other arithmetic  10.7 us (4%)
  starting transfers between devices  7.23 us (2%)
    ppermute x4, waiting for transfers between devices, passed_along(): return lax.ppermute(value, axis, pairs)  109 us
    psum x1, waiting for transfers between devices, per_device(): probe_total, norm_total = lax.psum((probe_sum, norm_sum), ('tile', 'pos'))  72.7 us
    psum x1, waiting for transfers between devices, per_device(): summed = lax.psum(upper_rows, 'pos')  40.2 us
    pallas_call x1, Pallas kernels, slots(): pl.pallas_call(slots_kernel, out_shape=(jax.ShapeDtypeStruct((planes + 1,...  39.3 us
    ppermute x4, starting transfers between devices, passed_along(): return lax.ppermute(value, axis, pairs)  7.15 us
  transfers between devices with their start and end apart: 6, of which 5 were waited for; matrix products, arithmetic and copies ran while one was open for 2% of the time, Pallas kernels for 0%

profile of v1, /device:TPU:23, one launch (start us, length us, event | category | flops | bytes accessed | tf_op | source)
XLA Modules:
  0.0 296.2 jit_solution(9873550965997928502)
XLA Ops:
  7.2 0.0 all-reduce.6.cloned.1.call-start
  7.2 2.0 collective-permute-start.1
  9.2 1.9 collective-permute-start
  11.8 0.0 copy-start.1
  11.8 0.0 copy-start.2
  11.8 0.0 copy-start.3
  11.8 0.0 copy-start.4
  11.9 0.0 copy-start.5
  11.9 0.0 copy-start.6
  11.9 41.9 %collective-permute-done.1 = f32[4,64,1024]{2,1,0:T(8,128)S(1)} collective-permute-done((f32[4,64,1024]{2,1,0:T(8,128)}, f32[4,64,1024]{2,1,0:T(8,128)S(1)}, u32[]{:S(2)}, u32[]{:S(2)}) %collective-permute-start.1) | collective-permute-done | bytes 1048608 | tf_op jit(solution)/shard_map/ppermute | solution.py:21
  53.8 22.5 %collective-permute-done = f32[4,64,1024]{2,1,0:T(8,128)S(1)} collective-permute-done((f32[4,64,1024]{2,1,0:T(8,128)}, f32[4,64,1024]{2,1,0:T(8,128)S(1)}, u32[]{:S(2)}, u32[]{:S(2)}) %collective-permute-start) | collective-permute-done | bytes 1048608 | tf_op jit(solution)/shard_map/ppermute | solution.py:21
  76.3 1.4 pad_maximum_fusion.object_ref
  77.7 0.0 copy-done.1
  77.7 0.0 copy-done.2
  77.7 0.0 copy-done.3
  77.7 0.0 copy-done.4
  77.8 0.0 copy-done.5
  77.8 0.0 copy-done.6
  77.8 39.3 %slots.1 = (f32[5,192,1024]{2,1,0:T(8,128)S(1)}, f32[4,2,128,128]{3,2,1,0:T(8,128)}, f32[128,128]{1,0:T(8,128)}) custom-call(s32[8]{0:T(128)S(1)} %bitcast.10, s32[8]{0:T(128)S(1)} %bitcast.11, s32[1]{0:T(128)} %bitcast.8.count_ref, f32[4,192,1024]{2,1,0:T(8,128)S(1)} %pad_maximum_fusion.object_ref, f32[4,2,128,128]{3,2,1,0:T(8,128)S(1)} %copy-done.1, ...), custom_call_target="tpu_custom_call" | custom-call | tf_op jit(solution)/shard_map/slots/pallas_call | solution.py:174
  117.1 0.0 copy-start
  117.1 1.4 fusion.2
  118.5 0.8 copy-done
  119.3 1.9 collective-permute-start.2
  121.2 1.3 collective-permute-start.3
  122.5 0.0 all-reduce.6.cloned.1.call-update
  122.5 0.0 all-reduce.4.cloned.1.call-start
  122.6 44.6 %collective-permute-done.2 = f32[5,64,1024]{2,1,0:T(8,128)S(1)} collective-permute-done((f32[5,64,1024]{2,1,0:T(8,128)}, f32[5,64,1024]{2,1,0:T(8,128)S(1)}, u32[]{:S(2)}, u32[]{:S(2)}) %collective-permute-start.2) | collective-permute-done | bytes 1310752 | tf_op jit(solution)/shard_map/ppermute | solution.py:21
  167.2 0.0 collective-permute-done.3
  167.2 3.2 %add_add_fusion = f32[5,64,1024]{2,1,0:T(8,128)} fusion(f32[5,64,1024]{2,1,0:T(8,128)} %collective-permute-done.3, f32[5,64,1024]{2,1,0:T(8,128)S(1)} %collective-permute-done.2, f32[5,192,1024]{2,1,0:T(8,128)} %copy-done), kind=kLoop, calls=%fused_computation.1 | loop fusion | flops 655360 | bytes 5242880 | tf_op jit(solution)/shard_map/add | solution.py:211
  170.4 0.0 all-reduce.4.cloned.1.call-update
  170.4 72.7 %all-reduce.6.cloned.1.call-done = (f32[4,2,128,128]{3,2,1,0:T(8,128)}, f32[128,128]{1,0:T(8,128)}) async-done(((f32[4,2,128,128]{3,2,1,0:T(8,128)}, f32[128,128]{1,0:T(8,128)}), (f32[4,2,128,128]{3,2,1,0:T(8,128)}, f32[128,128]{1,0:T(8,128)})) %all-reduce.6.cloned.1.call-update) | async-done | bytes 589840 | tf_op jit(solution)/shard_map/psum | solution.py:215
  243.1 0.8 broadcast_add_fusion
  244.0 1.9 multiply_divide_fusion
  245.8 40.2 %all-reduce.4.cloned.1.call-done = f32[5,64,1024]{2,1,0:T(8,128)} async-done(((f32[5,64,1024]{2,1,0:T(8,128)}), f32[5,64,1024]{2,1,0:T(8,128)}) %all-reduce.4.cloned.1.call-update) | async-done | bytes 1310736 | tf_op jit(solution)/shard_map/psum | solution.py:212
  286.0 1.0 fusion.1
  287.0 2.4 fusion
Async XLA Ops:
  7.2 235.9 %all-reduce.6.cloned.1.call-start = ((), (), s32[]{:S(2)}) async-start(), calls=%async_computation.1 | async-start | bytes 1179648 | tf_op jit(solution)/shard_map/psum | solution.py:215
  7.2 46.6 %collective-permute-start.1 = (f32[4,64,1024]{2,1,0:T(8,128)}, f32[4,64,1024]{2,1,0:T(8,128)S(1)}, u32[]{:S(2)}, u32[]{:S(2)}) collective-permute-start(f32[4,64,1024]{2,1,0:T(8,128)} %bitcast.13), channel_id=1, source_target_pairs={{8,0},{12,4},{9,1},{13,5},{10,2},{14,6},{11,3},{15,7},{24,16},{28,... | collective-permute-start | bytes 3145736 | tf_op jit(solution)/shard_map/ppermute | solution.py:21
  9.2 67.0 %collective-permute-start = (f32[4,64,1024]{2,1,0:T(8,128)}, f32[4,64,1024]{2,1,0:T(8,128)S(1)}, u32[]{:S(2)}, u32[]{:S(2)}) collective-permute-start(f32[4,64,1024]{2,1,0:T(8,128)} %bitcast.14), channel_id=1, source_target_pairs={{4,0},{8,4},{12,8},{5,1},{9,5},{13,9},{6,2},{10,6},{14,10},{7,3},{... | collective-permute-start | bytes 3145736 | tf_op jit(solution)/shard_map/ppermute | solution.py:21
  11.8 65.9 %copy-start.1 = (f32[4,2,128,128]{3,2,1,0:T(8,128)S(1)}, f32[4,2,128,128]{3,2,1,0:T(8,128)}, u32[]{:S(2)}) copy-start(f32[4,2,128,128]{3,2,1,0:T(8,128)} %probe_ref.1) | copy-start | bytes 1572868
  11.8 65.9 %copy-start.2 = (f32[1,1,8,128,128]{4,3,2,1,0:T(8,128)S(1)}, f32[1,1,8,128,128]{4,3,2,1,0:T(8,128)}, u32[]{:S(2)}) copy-start(f32[1,1,8,128,128]{4,3,2,1,0:T(8,128)} %param.10) | copy-start | bytes 1572868
  11.8 65.9 %copy-start.3 = (bf16[4,256,256]{2,1,0:T(8,128)(2,1)S(1)}, bf16[4,256,256]{2,1,0:T(8,128)(2,1)}, u32[]{:S(2)}) copy-start(bf16[4,256,256]{2,1,0:T(8,128)(2,1)} %constant.10.clone.low_ref) | copy-start | bytes 1572868
  11.8 65.9 %copy-start.4 = (bf16[4,256,256]{2,1,0:T(8,128)(2,1)S(1)}, bf16[4,256,256]{2,1,0:T(8,128)(2,1)}, u32[]{:S(2)}) copy-start(bf16[4,256,256]{2,1,0:T(8,128)(2,1)} %constant.3.clone.high_ref) | copy-start | bytes 1572868
  11.9 65.9 %copy-start.5 = (s32[1,1,8]{2,1,0:T(1,128)S(1)}, s32[1,1,8]{2,1,0:T(1,128)}, u32[]{:S(2)}) copy-start(s32[1,1,8]{2,1,0:T(1,128)} %param.11) | copy-start | bytes 100
  11.9 65.9 %copy-start.6 = (s32[1,1,8]{2,1,0:T(1,128)S(1)}, s32[1,1,8]{2,1,0:T(1,128)}, u32[]{:S(2)}) copy-start(s32[1,1,8]{2,1,0:T(1,128)} %param.12) | copy-start | bytes 100
  117.1 2.2 copy-start
  119.3 47.9 %collective-permute-start.2 = (f32[5,64,1024]{2,1,0:T(8,128)}, f32[5,64,1024]{2,1,0:T(8,128)S(1)}, u32[]{:S(2)}, u32[]{:S(2)}) collective-permute-start(f32[5,64,1024]{2,1,0:T(8,128)} %get-tuple-element.10), channel_id=1, source_target_pairs={{0,4},{4,8},{8,12},{1,5},{5,9},{9,13},{2,6},{6,10},{10,14},{3,7},{... | collective-permute-start | bytes 3932168 | tf_op jit(solution)/shard_map/ppermute | solution.py:21
  121.2 46.0 %collective-permute-start.3 = (f32[5,64,1024]{2,1,0:T(8,128)S(1)}, f32[5,64,1024]{2,1,0:T(8,128)}, u32[]{:S(2)}, u32[]{:S(2)}) collective-permute-start(f32[5,64,1024]{2,1,0:T(8,128)S(1)} %get-tuple-element.11), channel_id=1, source_target_pairs={{0,8},{4,12},{1,9},{5,13},{2,10},{6,14},{3,11},{7,15},{16,24},{20,... | collective-permute-start | bytes 3932168 | tf_op jit(solution)/shard_map/ppermute | solution.py:21
  122.5 163.5 %all-reduce.4.cloned.1.call-start = ((), (), s32[]{:S(2)}) async-start(), calls=%async_computation | async-start | bytes 2621440 | tf_op jit(solution)/shard_map/psum | solution.py:212
Sparse Core Ops, SparseCore 0:
  122.7 120.4 all-reduce.5
  245.5 40.4 all-reduce.3

commit v2 on v1

--- a/solution.py
+++ b/solution.py
@@ -13,12 +13,6 @@
 RELAX = 1.0
 PROBE_RATE = 4.0
 MIB = 1024 * 1024
-
-
-def passed_along(value, axis, by):
-    devices = lax.axis_size(axis)
-    pairs = [(i, i + by) for i in range(devices) if 0 <= i + by < devices]
-    return lax.ppermute(value, axis, pairs)
 
 
 def block_tables(side):
@@ -73,13 +67,12 @@
 
 def slots_kernel(
     row_ref, col_ref, count_ref, object_ref, probe_ref, measured_ref, high_ref, low_ref,
-    stacked_ref, probe_sum_ref, norm_ref, light_ref, mid_ref, far_ref,
+    stacked_ref, sums_ref, light_ref, mid_ref, far_ref,
 ):
     modes, _, side, _ = probe_ref.shape
     width = object_ref.shape[2]
     stacked_ref[...] = jnp.zeros_like(stacked_ref)
-    probe_sum_ref[...] = jnp.zeros_like(probe_sum_ref)
-    norm_ref[...] = jnp.zeros_like(norm_ref)
+    sums_ref[...] = jnp.zeros_like(sums_ref)
     light = jnp.zeros((side, side), jnp.float32)
     for m in range(modes):
         light = light + probe_ref[m, 0] * probe_ref[m, 0] + probe_ref[m, 1] * probe_ref[m, 1]
@@ -125,7 +118,7 @@
 
         upper = (patch(0), patch(1))
         lower = (patch(2), patch(3))
-        norm_ref[...] += upper[0] * upper[0] + upper[1] * upper[1]
+        sums_ref[2 * modes] += upper[0] * upper[0] + upper[1] * upper[1]
         place(4, light_ref[...])
         intensity = jnp.zeros((side, side), jnp.float32)
         for group in groups:
@@ -154,8 +147,8 @@
                 term = times_conj(grad, (probe_ref[m, 0], probe_ref[m, 1]))
                 upper_grad = (upper_grad[0] + term[0], upper_grad[1] + term[1])
                 term = times_conj(grad, upper)
-                probe_sum_ref[m, 0] += term[0]
-                probe_sum_ref[m, 1] += term[1]
+                sums_ref[2 * m] += term[0]
+                sums_ref[2 * m + 1] += term[1]
         place(0, upper_grad[0])
         place(1, upper_grad[1])
         place(2, lower_grad[0])
@@ -175,11 +168,10 @@
         slots_kernel,
         out_shape=(
             jax.ShapeDtypeStruct((planes + 1, ext_rows, width), jnp.float32),
-            jax.ShapeDtypeStruct(probe_modes.shape, jnp.float32),
-            jax.ShapeDtypeStruct((side, side), jnp.float32),
+            jax.ShapeDtypeStruct((2 * modes + 1, side, side), jnp.float32),
         ),
         in_specs=[smem] * 3 + [vmem] * 5,
-        out_specs=(vmem,) * 3,
+        out_specs=(vmem,) * 2,
         scratch_shapes=[
             pltpu.VMEM((side, side), jnp.float32),
             pltpu.VMEM(probe_modes.shape, jnp.float32),
@@ -190,14 +182,327 @@
     )(rows, cols, count, extended, probe_modes, measured, jnp.asarray(high), jnp.asarray(low))
 
 
+def flipped(index, bit):
+    return index + bit - 2 * bit * (index // bit % 2)
+
+
+def greet(peers):
+    barrier = pltpu.get_barrier_semaphore()
+    for peer in peers:
+        pl.semaphore_signal(barrier, inc=1, device_id=peer, device_id_type=pl.DeviceIdType.MESH)
+    pl.semaphore_wait(barrier, len(peers))
+
+
+def remote(source, target, send_sem, recv_sem, peer):
+    return pltpu.make_async_remote_copy(
+        src_ref=source,
+        dst_ref=target,
+        send_sem=send_sem,
+        recv_sem=recv_sem,
+        device_id=peer,
+        device_id_type=pl.DeviceIdType.MESH,
+    )
+
+
+class Places:
+    def __init__(self):
+        self.tiles = lax.axis_size("tile")
+        self.replicas = lax.axis_size("pos")
+        self.tile = lax.axis_index("tile")
+        self.own = lax.axis_index("pos")
+        self.near = flipped(self.own, 1)
+        self.far = flipped(self.own, 2)
+        self.cross = flipped(self.near, 2)
+        self.near_id = {"pos": self.near}
+        self.far_id = {"pos": self.far}
+        self.up_id = {"tile": lax.rem(self.tile + self.tiles - 1, self.tiles)}
+        self.down_id = {"tile": lax.rem(self.tile + 1, self.tiles)}
+
+    def rows(self, first, quarter, count):
+        return pl.ds(pl.multiple_of(first + quarter * count, 8), count)
+
+
+def halo_kernel(own_ref, ext_ref, tile_send, tile_recv, far_send, far_recv, near_send, near_recv):
+    at = Places()
+    strip = own_ref.shape[1]
+    part = strip // at.replicas
+    reach = ext_ref.shape[1] // strip - 1
+    greet([at.near_id, at.far_id, at.up_id, at.down_id])
+
+    def slot(k, quarter):
+        return ext_ref.at[:, at.rows(k * strip, quarter, part)]
+
+    def up(k):
+        if k == 1:
+            source = own_ref.at[:, at.rows(0, at.own, part)]
+        else:
+            source = slot(k - 1, at.own)
+        return remote(source, slot(k, at.own), tile_send.at[k - 1], tile_recv.at[k - 1], at.up_id)
+
+    def across(k, quarter):
+        return remote(slot(k, quarter), slot(k, quarter), far_send.at[k - 1], far_recv.at[k - 1], at.far_id)
+
+    def beside(k, which, quarter):
+        return remote(
+            slot(k, quarter), slot(k, quarter), near_send.at[k - 1, which], near_recv.at[k - 1, which], at.near_id
+        )
+
+    def sends(k):
+        return jnp.logical_and(at.tile > 0, at.tile + k - 1 < at.tiles)
+
+    @pl.when(sends(1))
+    def _():
+        up(1).start()
+
+    ext_ref[:, :strip] = own_ref[...]
+    for k in range(1, reach + 1):
+        @pl.when(at.tile + k >= at.tiles)
+        def _(k=k):
+            ext_ref[:, k * strip : (k + 1) * strip] = jnp.zeros(own_ref.shape, jnp.float32)
+
+    for k in range(1, reach + 1):
+        @pl.when(at.tile + k < at.tiles)
+        def _(k=k):
+            up(k).wait_recv()
+
+        if k < reach:
+            @pl.when(sends(k + 1))
+            def _(k=k):
+                up(k + 1).start()
+
+        @pl.when(at.tile + k < at.tiles)
+        def _(k=k):
+            across(k, at.own).start()
+            beside(k, 0, at.own).start()
+
+        if k > 1:
+            @pl.when(at.tile + k - 1 < at.tiles)
+            def _(k=k):
+                across(k - 1, at.far).wait_recv()
+                beside(k - 1, 1, at.far).start()
+
+    @pl.when(at.tile + reach < at.tiles)
+    def _():
+        across(reach, at.far).wait_recv()
+        beside(reach, 1, at.far).start()
+
+    for k in range(1, reach + 1):
+        @pl.when(sends(k))
+        def _(k=k):
+            up(k).wait_send()
+
+        @pl.when(at.tile + k < at.tiles)
+        def _(k=k):
+            beside(k, 0, at.near).wait_recv()
+            beside(k, 1, at.cross).wait_recv()
+            across(k, at.own).wait_send()
+            beside(k, 0, at.own).wait_send()
+            beside(k, 1, at.far).wait_send()
+
+
+def halo(own, reach, replicas):
+    planes, strip, width = own.shape
+    vmem = pl.BlockSpec(memory_space=pltpu.VMEM)
+    dma = pltpu.SemaphoreType.DMA
+    return pl.pallas_call(
+        halo_kernel,
+        out_shape=jax.ShapeDtypeStruct((planes, strip * (reach + 1), width), jnp.float32),
+        in_specs=[vmem],
+        out_specs=vmem,
+        scratch_shapes=[
+            dma((reach,)), dma((reach,)), dma((reach,)), dma((reach,)), dma((reach, 2)), dma((reach, 2))
+        ],
+        compiler_params=pltpu.CompilerParams(
+            collective_id=0, has_side_effects=True, vmem_limit_bytes=40 * MIB
+        ),
+        name="halo",
+    )(own)
+
+
+def reduce_kernel(
+    stacked_ref, sums_ref, object_ref, probe_ref,
+    near_land, far_out, far_land, kept, rim_land, sum_near, sum_far, sum_land, sum_steps, step_land,
+    near_send, near_recv, far_send, far_recv, rim_send, rim_recv,
+    pn_send, pn_recv, pf_send, pf_recv, step_send, step_recv, out_send, out_recv,
+):
+    at = Places()
+    strip = object_ref.shape[1]
+    part = strip // at.replicas
+    planes = object_ref.shape[0]
+    strips = stacked_ref.shape[1] // strip
+    sum_part = sums_ref.shape[1] // at.replicas
+    steps = at.tiles.bit_length() - 1
+    partners = [{"tile": flipped(at.tile, 2**i)} for i in range(steps)]
+    greet([at.near_id, at.far_id, at.up_id, at.down_id] + partners)
+
+    def rows(k, quarter):
+        return at.rows(k * strip, quarter, part)
+
+    def sum_rows(quarter):
+        return at.rows(0, quarter, sum_part)
+
+    def sum_beside(which, quarter):
+        return remote(
+            sums_ref.at[:, sum_rows(quarter)], sum_near.at[which], pn_send.at[which], pn_recv.at[which], at.near_id
+        )
+
+    def beside(k, which, quarter):
+        return remote(
+            stacked_ref.at[:, rows(k, quarter)], near_land.at[k, which],
+            near_send.at[k, which], near_recv.at[k, which], at.near_id,
+        )
+
+    def across(k):
+        return remote(far_out.at[k], far_land.at[k], far_send.at[k], far_recv.at[k], at.far_id)
+
+    def down(k):
+        return remote(kept.at[k], rim_land.at[k - 1], rim_send.at[k - 1], rim_recv.at[k - 1], at.down_id)
+
+    def step(i):
+        return remote(sum_steps.at[i], step_land.at[i], step_send.at[i], step_recv.at[i], partners[i])
+
+    sum_across = remote(sum_far, sum_land, pf_send, pf_recv, at.far_id)
+
+    sum_beside(1, at.cross).start()
+    sum_beside(0, at.near).start()
+    order = list(range(strips - 1, -1, -1))
+    for k in order:
+        beside(k, 1, at.cross).start()
+        beside(k, 0, at.near).start()
+
+    sum_beside(1, at.cross).wait_recv()
+    sum_far[...] = sums_ref[:, sum_rows(at.far)] + sum_near[1]
+    sum_across.start()
+    for k in order:
+        beside(k, 1, at.cross).wait_recv()
+        far_out[k] = stacked_ref[:, rows(k, at.far)] + near_land[k, 1]
+        across(k).start()
+    sum_beside(0, at.near).wait_recv()
+    total = sums_ref[:, sum_rows(at.own)] + sum_near[0]
+    sum_across.wait_recv()
+    sum_steps[0] = total + sum_land[...]
+    if steps:
+        step(0).start()
+    for k in order:
+        beside(k, 0, at.near).wait_recv()
+        across(k).wait_recv()
+        kept[k] = stacked_ref[:, rows(k, at.own)] + near_land[k, 0] + far_land[k]
+        if k < strips - 1:
+            @pl.when(at.tile > 0)
+            def _(k=k):
+                down(k + 1).wait_recv()
+                kept[k] += rim_land[k]
+
+        if k > 0:
+            @pl.when(at.tile < at.tiles - 1)
+            def _(k=k):
+                down(k).start()
+
+        i = strips - 1 - k
+        if i < min(steps, strips - 1):
+            step(i).wait_recv()
+            sum_steps[i + 1] = sum_steps[i] + step_land[i]
+            if i + 1 < steps:
+                step(i + 1).start()
+    for i in range(min(steps, strips - 1), steps):
+        step(i).wait_recv()
+        sum_steps[i + 1] = sum_steps[i] + step_land[i]
+        if i + 1 < steps:
+            step(i + 1).start()
+
+    def out(ref, which, lane, quarter, count, peer):
+        place = ref.at[:, at.rows(0, quarter, count)]
+        return remote(place, place, out_send.at[which, lane], out_recv.at[which, lane], peer)
+
+    probe_ref[:, sum_rows(at.own)] = (
+        -PROBE_RATE * sum_steps[steps, : 2 * (sums_ref.shape[0] // 2)] / (sum_steps[steps, 2 * (sums_ref.shape[0] // 2)] + RELAX)
+    )
+    outs = [(probe_ref, 0, sum_part), (object_ref, 1, part)]
+    ref, which, count = outs[0]
+    out(ref, which, 0, at.own, count, at.far_id).start()
+    out(ref, which, 1, at.own, count, at.near_id).start()
+    object_ref[:, rows(0, at.own)] = -kept[0, :planes] / (kept[0, planes] + RELAX)
+    ref, which, count = outs[1]
+    out(ref, which, 0, at.own, count, at.far_id).start()
+    out(ref, which, 1, at.own, count, at.near_id).start()
+    for ref, which, count in outs:
+        out(ref, which, 0, at.far, count, at.far_id).wait_recv()
+        out(ref, which, 2, at.far, count, at.near_id).start()
+    for ref, which, count in outs:
+        out(ref, which, 1, at.near, count, at.near_id).wait_recv()
+        out(ref, which, 2, at.cross, count, at.near_id).wait_recv()
+        out(ref, which, 0, at.own, count, at.far_id).wait_send()
+        out(ref, which, 1, at.own, count, at.near_id).wait_send()
+        out(ref, which, 2, at.far, count, at.near_id).wait_send()
+
+    sum_beside(1, at.cross).wait_send()
+    sum_beside(0, at.near).wait_send()
+    sum_across.wait_send()
+    for k in order:
+        beside(k, 1, at.cross).wait_send()
+        beside(k, 0, at.near).wait_send()
+        across(k).wait_send()
+        if k > 0:
+            @pl.when(at.tile < at.tiles - 1)
+            def _(k=k):
+                down(k).wait_send()
+    for i in range(steps):
+        step(i).wait_send()
+
+
+def reduced(stacked, sums, strip, tiles, replicas):
+    planes, ext_rows, width = stacked.shape
+    strips = ext_rows // strip
+    part = strip // replicas
+    sum_planes, side, _ = sums.shape
+    sum_part = side // replicas
+    steps = tiles.bit_length() - 1
+    vmem = pl.BlockSpec(memory_space=pltpu.VMEM)
+    dma = pltpu.SemaphoreType.DMA
+    block = (planes, part, width)
+    sum_block = (sum_planes, sum_part, side)
+
+    def buffer(*shape):
+        return pltpu.VMEM(shape, jnp.float32)
+
+    return pl.pallas_call(
+        reduce_kernel,
+        out_shape=(
+            jax.ShapeDtypeStruct((planes - 1, strip, width), jnp.float32),
+            jax.ShapeDtypeStruct((sum_planes - 1, side, side), jnp.float32),
+        ),
+        in_specs=[vmem, vmem],
+        out_specs=(vmem, vmem),
+        scratch_shapes=[
+            buffer(strips, 2, *block),
+            buffer(strips, *block),
+            buffer(strips, *block),
+            buffer(strips, *block),
+            buffer(strips - 1, *block),
+            buffer(2, *sum_block),
+            buffer(*sum_block),
+            buffer(*sum_block),
+            buffer(steps + 1, *sum_block),
+            buffer(max(steps, 1), *sum_block),
+            dma((strips, 2)), dma((strips, 2)), dma((strips,)), dma((strips,)), dma((strips - 1,)), dma((strips - 1,)),
+            dma((2,)), dma((2,)), dma, dma, dma((max(steps, 1),)), dma((max(steps, 1),)), dma((2, 3)), dma((2, 3)),
+        ],
+        compiler_params=pltpu.CompilerParams(
+            collective_id=1, has_side_effects=True, vmem_limit_bytes=48 * MIB
+        ),
+        name="reduce",
+    )(stacked, sums)
+
+
 def per_device(object_field, probe_modes, measured, row_offset, col_offset, position_count):
     layers, _, strip_rows, width = object_field.shape
     side = probe_modes.shape[2]
     reach = side // strip_rows
+    tiles = lax.axis_size("tile")
+    replicas = lax.axis_size("pos")
     own = object_field.reshape(2 * layers, strip_rows, width)
-    below = [passed_along(own, "tile", -by) for by in range(1, reach + 1)]
-    extended = jnp.concatenate([own] + below, axis=1)
-    stacked, probe_sum, norm_sum = slots(
+    extended = halo(own, reach, replicas)
+    stacked, sums = slots(
         row_offset.reshape(-1),
         col_offset.reshape(-1),
         position_count.reshape(-1),
@@ -205,16 +510,8 @@
         probe_modes,
         measured.reshape(-1, side, side),
     )
-    upper_rows = stacked[:, :strip_rows]
-    for by in range(1, reach + 1):
-        rim_rows = stacked[:, by * strip_rows : (by + 1) * strip_rows]
-        upper_rows = upper_rows + passed_along(rim_rows, "tile", by)
-    summed = lax.psum(upper_rows, "pos")
-    update_flat = -summed[: 2 * layers] / (summed[2 * layers][None] + RELAX)
-    object_update = update_flat.reshape(layers, 2, strip_rows, width)
-    probe_total, norm_total = lax.psum((probe_sum, norm_sum), ("tile", "pos"))
-    probe_update = -PROBE_RATE * probe_total / (norm_total[None, None] + RELAX)
-    return (object_update, probe_update)
+    object_flat, probe_flat = reduced(stacked, sums, strip_rows, tiles, replicas)
+    return object_flat.reshape(object_field.shape), probe_flat.reshape(probe_modes.shape)
 
 
 def solution(mesh):

time: 300 us -> 115 us (0.38)
  waiting for transfers between devices: 222 us -> 0 us
  Pallas kernels: 39.3 us -> 109 us
  between operations: 14.8 us -> 1.4 us
  other arithmetic: 10.7 us -> 0 us
  starting transfers between devices: 7.23 us -> 0 us
    psum x2 -> x0, waiting for transfers between devices: 113 us -> none  [the longest x1 72.7 us: per_device(): probe_total, norm_total = lax.psum((probe_sum, norm_sum), ('tile', 'pos'))]
    ppermute x4 -> x0, waiting for transfers between devices: 109 us -> none  [passed_along(): return lax.ppermute(value, axis, pairs)]
    pallas_call x0 -> x2, Pallas kernels: none -> 103 us  [the longest x1 86.3 us: reduced(): pl.pallas_call(reduce_kernel, out_shape=(jax.ShapeDtypeStruct((planes - 1...]
    pallas_call x1, Pallas kernels: 39.3 us -> 5.65 us  [slots(): pl.pallas_call(slots_kernel, out_shape=(jax.ShapeDtypeStruct((planes + 1,...]
    ppermute x4 -> x0, starting transfers between devices: 7.15 us -> none  [passed_along(): return lax.ppermute(value, axis, pairs)]
    div x3 -> x0, other arithmetic: 5.22 us -> none  [the longest x2 3.34 us: per_device(): update_flat = -summed[:2 * layers] / (summed[2 * layers][None] + RELAX)]
    add x2 -> x0, other arithmetic: 4.03 us -> none  [the longest x1 3.18 us: per_device(): upper_rows = upper_rows + passed_along(rim_rows, 'tile', by)]
  transfers between devices with their start and end apart: 6 -> 0, of which waited for: 5 -> 0; matrix products, arithmetic and copies ran while one was open for 2% -> 0% of each run, Pallas kernels for 0% -> 0%
where the time goes in v2:
time: 115 us; the launch traced here: 113 us
  Pallas kernels  109 us (95%)
  local copies, waits for them, and re-layouts  3.01 us (3%)
  between operations  1.4 us (1%)
    pallas_call x1, Pallas kernels, reduced(): pl.pallas_call(reduce_kernel, out_shape=(jax.ShapeDtypeStruct((planes - 1...  86.3 us
    pallas_call x1, Pallas kernels, halo(): pl.pallas_call(halo_kernel, out_shape=jax.ShapeDtypeStruct((planes, strip...  17 us
    pallas_call x1, Pallas kernels, slots(): pl.pallas_call(slots_kernel, out_shape=(jax.ShapeDtypeStruct((planes + 1,...  5.65 us
    unnamed x16, local copies, waits for them, and re-layouts  3.01 us

profile of v2, /device:TPU:23, one launch (start us, length us, event | category | flops | bytes accessed | tf_op | source)
XLA Modules:
  0.0 113.3 jit_solution(7104719660599318487)
XLA Ops:
  0.6 0.0 copy-start.6
  0.6 0.0 copy-start.5
  1.3 0.0 copy-start
  1.3 1.2 %copy-done = f32[2,2,64,1024]{3,2,1,0:T(8,128)S(1)} copy-done((f32[2,2,64,1024]{3,2,1,0:T(8,128)S(1)}, f32[2,2,64,1024]{3,2,1,0:T(8,128)}, u32[]{:S(2)}) %copy-start) | copy-done | bytes 1048600
  2.5 0.0 copy-start.1
  2.5 0.0 copy-start.2
  2.5 0.0 copy-start.3
  2.5 0.0 copy-start.4
  2.6 17.0 %halo.1.object_ref = f32[4,192,1024]{2,1,0:T(8,128)S(1)} custom-call(f32[4,64,1024]{2,1,0:T(8,128)S(1)} %bitcast.9), custom_call_target="tpu_custom_call" | custom-call | tf_op jit(solution)/shard_map/halo/pallas_call | solution.py:307
  19.5 0.0 copy-done.6
  19.5 0.0 copy-done.5
  19.5 0.0 copy-done.1
  19.5 0.0 copy-done.2
  19.6 0.0 copy-done.3
  19.6 0.0 copy-done.4
  19.6 5.7 %slots.1 = (f32[5,192,1024]{2,1,0:T(8,128)S(1)}, f32[9,128,128]{2,1,0:T(8,128)S(1)}) custom-call(s32[8]{0:T(128)S(1)} %bitcast.12, s32[8]{0:T(128)S(1)} %bitcast.13, s32[1]{0:T(128)} %bitcast.7.count_ref, f32[4,192,1024]{2,1,0:T(8,128)S(1)} %halo.1.object_ref, f32[4,2,128,128]{3,2,1,0:T(8,128)S(1)} %copy-done.1, f32[8,128,128]{2,1,0:T(8,128)S(1)} %bitcast.10, ...), custom_call_target="tpu_custom_call" | custom-call | tf_op jit(solution)/shard_map/slots/pallas_call | solution.py:167
  25.2 86.3 %reduce.1 = (f32[4,64,1024]{2,1,0:T(8,128)S(1)}, f32[8,128,128]{2,1,0:T(8,128)S(1)}) custom-call(f32[5,192,1024]{2,1,0:T(8,128)S(1)} %get-tuple-element.6.stacked_ref, f32[9,128,128]{2,1,0:T(8,128)S(1)} %get-tuple-element.7.sums_ref), custom_call_target="tpu_custom_call" | custom-call | tf_op jit(solution)/shard_map/reduce/pallas_call | solution.py:468
  111.6 1.0 copy.13
  112.6 0.8 copy.14
Async XLA Ops:
  0.6 18.9 %copy-start.6 = (s32[1,1,8]{2,1,0:T(1,128)S(1)}, s32[1,1,8]{2,1,0:T(1,128)}, u32[]{:S(2)}) copy-start(s32[1,1,8]{2,1,0:T(1,128)} %param.12) | copy-start | bytes 100
  0.6 18.9 %copy-start.5 = (s32[1,1,8]{2,1,0:T(1,128)S(1)}, s32[1,1,8]{2,1,0:T(1,128)}, u32[]{:S(2)}) copy-start(s32[1,1,8]{2,1,0:T(1,128)} %param.11) | copy-start | bytes 100
  1.3 1.2 %copy-start = (f32[2,2,64,1024]{3,2,1,0:T(8,128)S(1)}, f32[2,2,64,1024]{3,2,1,0:T(8,128)}, u32[]{:S(2)}) copy-start(f32[2,2,64,1024]{3,2,1,0:T(8,128)} %param.8) | copy-start | bytes 3145732
  2.5 17.0 %copy-start.1 = (f32[4,2,128,128]{3,2,1,0:T(8,128)S(1)}, f32[4,2,128,128]{3,2,1,0:T(8,128)}, u32[]{:S(2)}) copy-start(f32[4,2,128,128]{3,2,1,0:T(8,128)} %probe_ref.1) | copy-start | bytes 1572868
  2.5 17.0 %copy-start.2 = (f32[1,1,8,128,128]{4,3,2,1,0:T(8,128)S(1)}, f32[1,1,8,128,128]{4,3,2,1,0:T(8,128)}, u32[]{:S(2)}) copy-start(f32[1,1,8,128,128]{4,3,2,1,0:T(8,128)} %param.10) | copy-start | bytes 1572868
  2.5 17.0 %copy-start.3 = (bf16[4,256,256]{2,1,0:T(8,128)(2,1)S(1)}, bf16[4,256,256]{2,1,0:T(8,128)(2,1)}, u32[]{:S(2)}) copy-start(bf16[4,256,256]{2,1,0:T(8,128)(2,1)} %constant.5.clone.low_ref) | copy-start | bytes 1572868
  2.5 17.0 %copy-start.4 = (bf16[4,256,256]{2,1,0:T(8,128)(2,1)S(1)}, bf16[4,256,256]{2,1,0:T(8,128)(2,1)}, u32[]{:S(2)}) copy-start(bf16[4,256,256]{2,1,0:T(8,128)(2,1)} %constant.4.clone.high_ref) | copy-start | bytes 1572868

commit v3 on v2

--- a/solution.py
+++ b/solution.py
@@ -66,7 +66,7 @@
 
 
 def slots_kernel(
-    row_ref, col_ref, count_ref, object_ref, probe_ref, measured_ref, high_ref, low_ref,
+    info_ref, object_ref, probe_ref, measured_ref, high_ref, low_ref,
     stacked_ref, sums_ref, light_ref, mid_ref, far_ref,
 ):
     modes, _, side, _ = probe_ref.shape
@@ -85,9 +85,18 @@
             fields, high_ref[table], low_ref[table], high_ref[conj_table], low_ref[conj_table]
         )
 
+    parity = lax.rem(lax.axis_index("pos"), 2)
+    count_even = info_ref[0, 2, 0]
+    count_all = count_even + info_ref[1, 2, 0]
+    half = (count_all + 1) // 2
+    first_slot = parity * half
+    last_slot = jnp.where(parity == 0, half, count_all)
+
     def visit(slot, carry):
-        row = row_ref[slot]
-        col = col_ref[slot]
+        second = (slot >= count_even).astype(jnp.int32)
+        within = slot - second * count_even
+        row = info_ref[second, 0, within]
+        col = info_ref[second, 1, within]
         base = pl.multiple_of(jnp.minimum(col // 128 * 128, width - 2 * 128), 128)
         offset = col - base
         lane = lax.broadcasted_iota(jnp.int32, (side + 8, 128), 1)
@@ -100,21 +109,21 @@
         rise = lax.rem(tall - shift, tall)
 
         def patch(plane):
-            first = object_ref[plane, pl.ds(start, tall), pl.ds(base, 128)]
-            second = object_ref[plane, pl.ds(start, tall), pl.ds(base + 128, 128)]
-            chosen = pltpu.roll(jnp.where(lane >= offset, first, second), back, 1)
+            left = object_ref[plane, pl.ds(start, tall), pl.ds(base, 128)]
+            right = object_ref[plane, pl.ds(start, tall), pl.ds(base + 128, 128)]
+            chosen = pltpu.roll(jnp.where(lane >= offset, left, right), back, 1)
             return pltpu.roll(chosen, rise, 0)[:side]
 
         def place(plane, value):
             value = jnp.concatenate([value, jnp.zeros((8, side), jnp.float32)], axis=0)
             value = pltpu.roll(pltpu.roll(value, ahead, 1), shift, 0)
             kept = lane >= offset
-            first = jnp.where(kept, value, 0.0)
-            second = jnp.where(kept, 0.0, value)
+            left = jnp.where(kept, value, 0.0)
+            right = jnp.where(kept, 0.0, value)
             at = (plane, pl.ds(start, tall), pl.ds(base, 128))
-            stacked_ref[at] = stacked_ref[at] + first
+            stacked_ref[at] = stacked_ref[at] + left
             at = (plane, pl.ds(start, tall), pl.ds(base + 128, 128))
-            stacked_ref[at] = stacked_ref[at] + second
+            stacked_ref[at] = stacked_ref[at] + right
 
         upper = (patch(0), patch(1))
         lower = (patch(2), patch(3))
@@ -132,7 +141,7 @@
                 far_ref[m, 0] = wave[0]
                 far_ref[m, 1] = wave[1]
                 intensity = intensity + wave[0] * wave[0] + wave[1] * wave[1]
-        misfit = 2.0 * (intensity - measured_ref[slot])
+        misfit = 2.0 * (intensity - measured_ref[second, within])
         zero = jnp.zeros((side, side), jnp.float32)
         lower_grad = (zero, zero)
         upper_grad = (zero, zero)
@@ -155,10 +164,10 @@
         place(3, lower_grad[1])
         return carry
 
-    lax.fori_loop(0, count_ref[0], visit, 0)
-
-
-def slots(rows, cols, count, extended, probe_modes, measured):
+    lax.fori_loop(first_slot, last_slot, visit, 0)
+
+
+def slots(info, extended, probe_modes, measured):
     modes, _, side, _ = probe_modes.shape
     high, low = block_tables(side)
     planes, ext_rows, width = extended.shape
@@ -170,7 +179,7 @@
             jax.ShapeDtypeStruct((planes + 1, ext_rows, width), jnp.float32),
             jax.ShapeDtypeStruct((2 * modes + 1, side, side), jnp.float32),
         ),
-        in_specs=[smem] * 3 + [vmem] * 5,
+        in_specs=[smem] + [vmem] * 5,
         out_specs=(vmem,) * 2,
         scratch_shapes=[
             pltpu.VMEM((side, side), jnp.float32),
@@ -179,7 +188,7 @@
         ],
         compiler_params=pltpu.CompilerParams(vmem_limit_bytes=40 * MIB),
         name="slots",
-    )(rows, cols, count, extended, probe_modes, measured, jnp.asarray(high), jnp.asarray(low))
+    )(info, extended, probe_modes, measured, jnp.asarray(high), jnp.asarray(low))
 
 
 def flipped(index, bit):
@@ -222,7 +231,10 @@
         return pl.ds(pl.multiple_of(first + quarter * count, 8), count)
 
 
-def halo_kernel(own_ref, ext_ref, tile_send, tile_recv, far_send, far_recv, near_send, near_recv):
+def halo_kernel(
+    own_ref, info_ref, measured_ref, ext_ref, info_pair, measured_pair,
+    tile_send, tile_recv, far_send, far_recv, near_send, near_recv, pair_send, pair_recv,
+):
     at = Places()
     strip = own_ref.shape[1]
     part = strip // at.replicas
@@ -254,6 +266,17 @@
     def _():
         up(1).start()
 
+    parity = lax.rem(at.own, 2)
+
+    def share(i, place):
+        source = (info_ref, measured_ref)[i]
+        pair = (info_pair, measured_pair)[i]
+        return remote(source, pair.at[place], pair_send.at[i], pair_recv.at[i], at.near_id)
+
+    share(0, parity).start()
+    share(1, parity).start()
+    info_pair[parity] = info_ref[...]
+    measured_pair[parity] = measured_ref[...]
     ext_ref[:, :strip] = own_ref[...]
     for k in range(1, reach + 1):
         @pl.when(at.tile + k >= at.tiles)
@@ -299,24 +322,33 @@
             beside(k, 0, at.own).wait_send()
             beside(k, 1, at.far).wait_send()
 
-
-def halo(own, reach, replicas):
+    for i in range(2):
+        share(i, 1 - parity).wait_recv()
+        share(i, parity).wait_send()
+
+
+def halo(own, info, measured, reach):
     planes, strip, width = own.shape
     vmem = pl.BlockSpec(memory_space=pltpu.VMEM)
     dma = pltpu.SemaphoreType.DMA
     return pl.pallas_call(
         halo_kernel,
-        out_shape=jax.ShapeDtypeStruct((planes, strip * (reach + 1), width), jnp.float32),
-        in_specs=[vmem],
-        out_specs=vmem,
+        out_shape=(
+            jax.ShapeDtypeStruct((planes, strip * (reach + 1), width), jnp.float32),
+            jax.ShapeDtypeStruct((2,) + info.shape, jnp.int32),
+            jax.ShapeDtypeStruct((2,) + measured.shape, jnp.float32),
+        ),
+        in_specs=[vmem] * 3,
+        out_specs=(vmem,) * 3,
         scratch_shapes=[
-            dma((reach,)), dma((reach,)), dma((reach,)), dma((reach,)), dma((reach, 2)), dma((reach, 2))
+            dma((reach,)), dma((reach,)), dma((reach,)), dma((reach,)), dma((reach, 2)), dma((reach, 2)),
+            dma((2,)), dma((2,)),
         ],
         compiler_params=pltpu.CompilerParams(
             collective_id=0, has_side_effects=True, vmem_limit_bytes=40 * MIB
         ),
         name="halo",
-    )(own)
+    )(own, info, measured)
 
 
 def reduce_kernel(
@@ -501,15 +533,14 @@
     tiles = lax.axis_size("tile")
     replicas = lax.axis_size("pos")
     own = object_field.reshape(2 * layers, strip_rows, width)
-    extended = halo(own, reach, replicas)
-    stacked, sums = slots(
-        row_offset.reshape(-1),
-        col_offset.reshape(-1),
-        position_count.reshape(-1),
-        extended,
-        probe_modes,
-        measured.reshape(-1, side, side),
+    slots_here = row_offset.size
+    count = jnp.broadcast_to(position_count.reshape(1, 1), (1, slots_here))
+    info = jnp.concatenate(
+        [row_offset.reshape(1, -1), col_offset.reshape(1, -1), count], axis=0
     )
+    info = jnp.pad(info, ((0, 5), (0, 128 - slots_here)))
+    extended, info_pair, measured_pair = halo(own, info, measured.reshape(-1, side, side), reach)
+    stacked, sums = slots(info_pair, extended, probe_modes, measured_pair)
     object_flat, probe_flat = reduced(stacked, sums, strip_rows, tiles, replicas)
     return object_flat.reshape(object_field.shape), probe_flat.reshape(probe_modes.shape)
 

time: 115 us -> 108 us (0.939); the launches traced: 113 us -> 109 us
  Pallas kernels: 109 us -> 99.9 us
  local copies, waits for them, and re-layouts: 3.01 us -> 7.23 us
    pallas_call x1, Pallas kernels: 86.3 us -> 72.4 us  [reduced(): pl.pallas_call(reduce_kernel, out_shape=(jax.ShapeDtypeStruct((planes - 1...]
    pallas_call x1, Pallas kernels: 5.65 us -> 10.6 us  [slots(): pl.pallas_call(slots_kernel, out_shape=(jax.ShapeDtypeStruct((planes + 1,...]
    unnamed x16 -> x12, local copies, waits for them, and re-layouts: 3.01 us -> 7.15 us
where the time goes in v3:
time: 108 us; the launch traced here: 109 us
  Pallas kernels  99.9 us (92%)
  local copies, waits for them, and re-layouts  7.23 us (7%)
  between operations  1.31 us (1%)
    pallas_call x1, Pallas kernels, reduced(): pl.pallas_call(reduce_kernel, out_shape=(jax.ShapeDtypeStruct((planes - 1...  72.4 us
    pallas_call x1, Pallas kernels, halo(): pl.pallas_call(halo_kernel, out_shape=(jax.ShapeDtypeStruct((planes, stri...  16.9 us
    pallas_call x1, Pallas kernels, slots(): pl.pallas_call(slots_kernel, out_shape=(jax.ShapeDtypeStruct((planes + 1,...  10.6 us
    unnamed x12, local copies, waits for them, and re-layouts  7.15 us

profile of v3, /device:TPU:23, one launch (start us, length us, event | category | flops | bytes accessed | tf_op | source)
XLA Modules:
  0.0 109.2 jit_solution(16919458240531491032)
XLA Ops:
  1.3 0.1 pad.7.clone
  1.4 0.7 add_add_fusion
  2.1 0.0 copy-start
  2.1 1.2 %copy-done = f32[2,2,64,1024]{3,2,1,0:T(8,128)S(1)} copy-done((f32[2,2,64,1024]{3,2,1,0:T(8,128)S(1)}, f32[2,2,64,1024]{3,2,1,0:T(8,128)}, u32[]{:S(2)}) %copy-start) | copy-done | bytes 1048600
  3.3 0.0 copy-start.1
  3.3 1.0 copy-done.1
  4.4 16.9 %halo.1 = (f32[4,192,1024]{2,1,0:T(8,128)S(1)}, s32[2,8,128]{2,1,0:T(8,128)S(1)}, f32[2,8,128,128]{3,2,1,0:T(8,128)S(1)}) custom-call(f32[4,64,1024]{2,1,0:T(8,128)S(1)} %bitcast.10, s32[8,128]{1,0:T(8,128)S(1)} %pad.4.info_ref, f32[8,128,128]{2,1,0:T(8,128)S(1)} %bitcast.12), custom_call_target="tpu_custom_call" | custom-call | tf_op jit(solution)/shard_map/halo/pallas_call | solution.py:334
  21.3 0.0 copy-start.2
  21.3 1.0 copy-done.2
  22.4 0.0 copy-start.3
  22.4 1.0 copy-done.3
  23.4 0.0 copy-start.4
  23.4 1.0 copy-done.4
  24.4 10.6 %slots.1 = (f32[5,192,1024]{2,1,0:T(8,128)S(1)}, f32[9,128,128]{2,1,0:T(8,128)S(1)}) custom-call(s32[2,8,128]{2,1,0:T(8,128)S(1)} %get-tuple-element.9.info_ref, f32[4,192,1024]{2,1,0:T(8,128)S(1)} %get-tuple-element.10.object_ref, f32[4,2,128,128]{3,2,1,0:T(8,128)S(1)} %copy-done.2, f32[2,8,128,128]{3,2,1,0:T(8,128)S(1)} %get-tuple-element.11.measured_ref, ...), custom_call_target="tpu_custom_call" | custom-call | tf_op jit(solution)/shard_map/slots/pallas_call | solution.py:176
  35.1 72.4 %reduce.1 = (f32[4,64,1024]{2,1,0:T(8,128)S(1)}, f32[8,128,128]{2,1,0:T(8,128)S(1)}) custom-call(f32[5,192,1024]{2,1,0:T(8,128)S(1)} %get-tuple-element.12.stacked_ref, f32[9,128,128]{2,1,0:T(8,128)S(1)} %get-tuple-element.13.sums_ref), custom_call_target="tpu_custom_call" | custom-call | tf_op jit(solution)/shard_map/reduce/pallas_call | solution.py:500
  107.5 1.0 copy.13
  108.4 0.8 copy.14
  (1 shorter events, 0.0 us)
Async XLA Ops:
  2.1 1.2 %copy-start = (f32[2,2,64,1024]{3,2,1,0:T(8,128)S(1)}, f32[2,2,64,1024]{3,2,1,0:T(8,128)}, u32[]{:S(2)}) copy-start(f32[2,2,64,1024]{3,2,1,0:T(8,128)} %param.8) | copy-start | bytes 3145732
  3.3 1.0 copy-start.1
  21.3 1.0 copy-start.2
  22.4 1.0 copy-start.3
  23.4 1.0 copy-start.4

commit v4 on v3

--- a/solution.py
+++ b/solution.py
@@ -13,6 +13,7 @@
 RELAX = 1.0
 PROBE_RATE = 4.0
 MIB = 1024 * 1024
+CUTS = 2
 
 
 def block_tables(side):
@@ -77,7 +78,7 @@
     for m in range(modes):
         light = light + probe_ref[m, 0] * probe_ref[m, 0] + probe_ref[m, 1] * probe_ref[m, 1]
     light_ref[...] = light
-    groups = [list(range(m, min(m + 2, modes))) for m in range(0, modes, 2)]
+    groups = [list(range(modes))]
     prop, prop_c, four, four_c = range(4)
 
     def apply(fields, table, conj_table):
@@ -241,30 +242,38 @@
     reach = ext_ref.shape[1] // strip - 1
     greet([at.near_id, at.far_id, at.up_id, at.down_id])
 
-    def slot(k, quarter):
-        return ext_ref.at[:, at.rows(k * strip, quarter, part)]
-
-    def up(k):
+    def cols(j):
+        piece = own_ref.shape[2] // CUTS
+        return pl.ds(j * piece, piece)
+
+    def slot(k, j, quarter):
+        return ext_ref.at[:, at.rows(k * strip, quarter, part), cols(j)]
+
+    def up(k, j):
+        i = (k - 1) * CUTS + j
         if k == 1:
-            source = own_ref.at[:, at.rows(0, at.own, part)]
+            source = own_ref.at[:, at.rows(0, at.own, part), cols(j)]
         else:
-            source = slot(k - 1, at.own)
-        return remote(source, slot(k, at.own), tile_send.at[k - 1], tile_recv.at[k - 1], at.up_id)
-
-    def across(k, quarter):
-        return remote(slot(k, quarter), slot(k, quarter), far_send.at[k - 1], far_recv.at[k - 1], at.far_id)
-
-    def beside(k, which, quarter):
-        return remote(
-            slot(k, quarter), slot(k, quarter), near_send.at[k - 1, which], near_recv.at[k - 1, which], at.near_id
-        )
+            source = slot(k - 1, j, at.own)
+        return remote(source, slot(k, j, at.own), tile_send.at[i], tile_recv.at[i], at.up_id)
+
+    def across(k, j, quarter):
+        i = (k - 1) * CUTS + j
+        place = slot(k, j, quarter)
+        return remote(place, place, far_send.at[i], far_recv.at[i], at.far_id)
+
+    def beside(k, j, which, quarter):
+        i = (k - 1) * CUTS + j
+        place = slot(k, j, quarter)
+        return remote(place, place, near_send.at[i, which], near_recv.at[i, which], at.near_id)
 
     def sends(k):
         return jnp.logical_and(at.tile > 0, at.tile + k - 1 < at.tiles)
 
     @pl.when(sends(1))
     def _():
-        up(1).start()
+        for j in range(CUTS):
+            up(1, j).start()
 
     parity = lax.rem(at.own, 2)
 
@@ -283,44 +292,45 @@
         def _(k=k):
             ext_ref[:, k * strip : (k + 1) * strip] = jnp.zeros(own_ref.shape, jnp.float32)
 
-    for k in range(1, reach + 1):
+    items = [(k, j) for k in range(1, reach + 1) for j in range(CUTS)]
+
+    def second_hop(k, j):
         @pl.when(at.tile + k < at.tiles)
-        def _(k=k):
-            up(k).wait_recv()
+        def _():
+            across(k, j, at.far).wait_recv()
+            beside(k, j, 1, at.far).start()
+
+    for i, (k, j) in enumerate(items):
+        @pl.when(at.tile + k < at.tiles)
+        def _(k=k, j=j):
+            up(k, j).wait_recv()
 
         if k < reach:
             @pl.when(sends(k + 1))
-            def _(k=k):
-                up(k + 1).start()
+            def _(k=k, j=j):
+                up(k + 1, j).start()
 
         @pl.when(at.tile + k < at.tiles)
-        def _(k=k):
-            across(k, at.own).start()
-            beside(k, 0, at.own).start()
-
-        if k > 1:
-            @pl.when(at.tile + k - 1 < at.tiles)
-            def _(k=k):
-                across(k - 1, at.far).wait_recv()
-                beside(k - 1, 1, at.far).start()
-
-    @pl.when(at.tile + reach < at.tiles)
-    def _():
-        across(reach, at.far).wait_recv()
-        beside(reach, 1, at.far).start()
-
-    for k in range(1, reach + 1):
+        def _(k=k, j=j):
+            across(k, j, at.own).start()
+            beside(k, j, 0, at.own).start()
+
+        if i > 0:
+            second_hop(*items[i - 1])
+    second_hop(*items[-1])
+
+    for k, j in items:
         @pl.when(sends(k))
-        def _(k=k):
-            up(k).wait_send()
+        def _(k=k, j=j):
+            up(k, j).wait_send()
 
         @pl.when(at.tile + k < at.tiles)
-        def _(k=k):
-            beside(k, 0, at.near).wait_recv()
-            beside(k, 1, at.cross).wait_recv()
-            across(k, at.own).wait_send()
-            beside(k, 0, at.own).wait_send()
-            beside(k, 1, at.far).wait_send()
+        def _(k=k, j=j):
+            beside(k, j, 0, at.near).wait_recv()
+            beside(k, j, 1, at.cross).wait_recv()
+            across(k, j, at.own).wait_send()
+            beside(k, j, 0, at.own).wait_send()
+            beside(k, j, 1, at.far).wait_send()
 
     for i in range(2):
         share(i, 1 - parity).wait_recv()
@@ -341,7 +351,7 @@
         in_specs=[vmem] * 3,
         out_specs=(vmem,) * 3,
         scratch_shapes=[
-            dma((reach,)), dma((reach,)), dma((reach,)), dma((reach,)), dma((reach, 2)), dma((reach, 2)),
+            *[dma((reach * CUTS,))] * 4, *[dma((reach * CUTS, 2))] * 2,
             dma((2,)), dma((2,)),
         ],
         compiler_params=pltpu.CompilerParams(
@@ -378,106 +388,126 @@
             sums_ref.at[:, sum_rows(quarter)], sum_near.at[which], pn_send.at[which], pn_recv.at[which], at.near_id
         )
 
-    def beside(k, which, quarter):
+    width = stacked_ref.shape[2]
+
+    def cols(j):
+        return pl.ds(j * (width // CUTS), width // CUTS)
+
+    def beside(k, j, which, quarter):
         return remote(
-            stacked_ref.at[:, rows(k, quarter)], near_land.at[k, which],
-            near_send.at[k, which], near_recv.at[k, which], at.near_id,
+            stacked_ref.at[:, rows(k, quarter), cols(j)], near_land.at[k, j, which],
+            near_send.at[k, j, which], near_recv.at[k, j, which], at.near_id,
         )
 
-    def across(k):
-        return remote(far_out.at[k], far_land.at[k], far_send.at[k], far_recv.at[k], at.far_id)
-
-    def down(k):
-        return remote(kept.at[k], rim_land.at[k - 1], rim_send.at[k - 1], rim_recv.at[k - 1], at.down_id)
+    def across(k, j):
+        return remote(
+            far_out.at[k, j], far_land.at[k, j], far_send.at[k, j], far_recv.at[k, j], at.far_id
+        )
+
+    def down(k, j):
+        return remote(
+            kept.at[k, j], rim_land.at[k - 1, j], rim_send.at[k - 1, j], rim_recv.at[k - 1, j], at.down_id
+        )
 
     def step(i):
         return remote(sum_steps.at[i], step_land.at[i], step_send.at[i], step_recv.at[i], partners[i])
 
+    def object_out(j, lane, quarter, peer):
+        place = object_ref.at[:, rows(0, quarter), cols(j)]
+        return remote(place, place, out_send.at[1 + j, lane], out_recv.at[1 + j, lane], peer)
+
+    def probe_out(lane, quarter, peer):
+        place = probe_ref.at[:, sum_rows(quarter)]
+        return remote(place, place, out_send.at[0, lane], out_recv.at[0, lane], peer)
+
+    def probe_update():
+        last = sums_ref.shape[0] - 1
+        update = -PROBE_RATE * sum_steps[steps, :last] / (sum_steps[steps, last] + RELAX)
+        probe_ref[:, sum_rows(at.own)] = update
+        probe_out(0, at.own, at.far_id).start()
+        probe_out(1, at.own, at.near_id).start()
+
     sum_across = remote(sum_far, sum_land, pf_send, pf_recv, at.far_id)
 
     sum_beside(1, at.cross).start()
     sum_beside(0, at.near).start()
-    order = list(range(strips - 1, -1, -1))
-    for k in order:
-        beside(k, 1, at.cross).start()
-        beside(k, 0, at.near).start()
+    order = [(k, j) for k in range(strips - 1, -1, -1) for j in range(CUTS)]
+    for k, j in order:
+        beside(k, j, 1, at.cross).start()
+    for k, j in order:
+        beside(k, j, 0, at.near).start()
 
     sum_beside(1, at.cross).wait_recv()
     sum_far[...] = sums_ref[:, sum_rows(at.far)] + sum_near[1]
     sum_across.start()
-    for k in order:
-        beside(k, 1, at.cross).wait_recv()
-        far_out[k] = stacked_ref[:, rows(k, at.far)] + near_land[k, 1]
-        across(k).start()
+    for k, j in order:
+        beside(k, j, 1, at.cross).wait_recv()
+        far_out[k, j] = stacked_ref[:, rows(k, at.far), cols(j)] + near_land[k, j, 1]
+        across(k, j).start()
     sum_beside(0, at.near).wait_recv()
     total = sums_ref[:, sum_rows(at.own)] + sum_near[0]
     sum_across.wait_recv()
     sum_steps[0] = total + sum_land[...]
     if steps:
         step(0).start()
-    for k in order:
-        beside(k, 0, at.near).wait_recv()
-        across(k).wait_recv()
-        kept[k] = stacked_ref[:, rows(k, at.own)] + near_land[k, 0] + far_land[k]
+    for k, j in order:
+        beside(k, j, 0, at.near).wait_recv()
+        across(k, j).wait_recv()
+        kept[k, j] = stacked_ref[:, rows(k, at.own), cols(j)] + near_land[k, j, 0] + far_land[k, j]
         if k < strips - 1:
             @pl.when(at.tile > 0)
-            def _(k=k):
-                down(k + 1).wait_recv()
-                kept[k] += rim_land[k]
+            def _(k=k, j=j):
+                down(k + 1, j).wait_recv()
+                kept[k, j] += rim_land[k, j]
 
         if k > 0:
             @pl.when(at.tile < at.tiles - 1)
-            def _(k=k):
-                down(k).start()
+            def _(k=k, j=j):
+                down(k, j).start()
+        else:
+            update = -kept[0, j, :planes] / (kept[0, j, planes] + RELAX)
+            object_ref[:, rows(0, at.own), cols(j)] = update
+            object_out(j, 0, at.own, at.far_id).start()
+            object_out(j, 1, at.own, at.near_id).start()
 
         i = strips - 1 - k
-        if i < min(steps, strips - 1):
+        if j == CUTS - 1 and i < min(steps, strips - 1):
             step(i).wait_recv()
             sum_steps[i + 1] = sum_steps[i] + step_land[i]
             if i + 1 < steps:
                 step(i + 1).start()
+            elif i + 1 == steps:
+                probe_update()
     for i in range(min(steps, strips - 1), steps):
         step(i).wait_recv()
         sum_steps[i + 1] = sum_steps[i] + step_land[i]
         if i + 1 < steps:
             step(i + 1).start()
 
-    def out(ref, which, lane, quarter, count, peer):
-        place = ref.at[:, at.rows(0, quarter, count)]
-        return remote(place, place, out_send.at[which, lane], out_recv.at[which, lane], peer)
-
-    probe_ref[:, sum_rows(at.own)] = (
-        -PROBE_RATE * sum_steps[steps, : 2 * (sums_ref.shape[0] // 2)] / (sum_steps[steps, 2 * (sums_ref.shape[0] // 2)] + RELAX)
-    )
-    outs = [(probe_ref, 0, sum_part), (object_ref, 1, part)]
-    ref, which, count = outs[0]
-    out(ref, which, 0, at.own, count, at.far_id).start()
-    out(ref, which, 1, at.own, count, at.near_id).start()
-    object_ref[:, rows(0, at.own)] = -kept[0, :planes] / (kept[0, planes] + RELAX)
-    ref, which, count = outs[1]
-    out(ref, which, 0, at.own, count, at.far_id).start()
-    out(ref, which, 1, at.own, count, at.near_id).start()
-    for ref, which, count in outs:
-        out(ref, which, 0, at.far, count, at.far_id).wait_recv()
-        out(ref, which, 2, at.far, count, at.near_id).start()
-    for ref, which, count in outs:
-        out(ref, which, 1, at.near, count, at.near_id).wait_recv()
-        out(ref, which, 2, at.cross, count, at.near_id).wait_recv()
-        out(ref, which, 0, at.own, count, at.far_id).wait_send()
-        out(ref, which, 1, at.own, count, at.near_id).wait_send()
-        out(ref, which, 2, at.far, count, at.near_id).wait_send()
+    if steps > strips - 1 or steps == 0:
+        probe_update()
+    outs = [probe_out] + [functools.partial(object_out, j) for j in range(CUTS)]
+    for out in outs:
+        out(0, at.far, at.far_id).wait_recv()
+        out(2, at.far, at.near_id).start()
+    for out in outs:
+        out(1, at.near, at.near_id).wait_recv()
+        out(2, at.cross, at.near_id).wait_recv()
+        out(0, at.own, at.far_id).wait_send()
+        out(1, at.own, at.near_id).wait_send()
+        out(2, at.far, at.near_id).wait_send()
 
     sum_beside(1, at.cross).wait_send()
     sum_beside(0, at.near).wait_send()
     sum_across.wait_send()
-    for k in order:
-        beside(k, 1, at.cross).wait_send()
-        beside(k, 0, at.near).wait_send()
-        across(k).wait_send()
+    for k, j in order:
+        beside(k, j, 1, at.cross).wait_send()
+        beside(k, j, 0, at.near).wait_send()
+        across(k, j).wait_send()
         if k > 0:
             @pl.when(at.tile < at.tiles - 1)
-            def _(k=k):
-                down(k).wait_send()
+            def _(k=k, j=j):
+                down(k, j).wait_send()
     for i in range(steps):
         step(i).wait_send()
 
@@ -491,7 +521,7 @@
     steps = tiles.bit_length() - 1
     vmem = pl.BlockSpec(memory_space=pltpu.VMEM)
     dma = pltpu.SemaphoreType.DMA
-    block = (planes, part, width)
+    block = (planes, part, width // CUTS)
     sum_block = (sum_planes, sum_part, side)
 
     def buffer(*shape):
@@ -506,18 +536,18 @@
         in_specs=[vmem, vmem],
         out_specs=(vmem, vmem),
         scratch_shapes=[
-            buffer(strips, 2, *block),
-            buffer(strips, *block),
-            buffer(strips, *block),
-            buffer(strips, *block),
-            buffer(strips - 1, *block),
+            buffer(strips, CUTS, 2, *block),
+            buffer(strips, CUTS, *block),
+            buffer(strips, CUTS, *block),
+            buffer(strips, CUTS, *block),
+            buffer(strips - 1, CUTS, *block),
             buffer(2, *sum_block),
             buffer(*sum_block),
             buffer(*sum_block),
             buffer(steps + 1, *sum_block),
             buffer(max(steps, 1), *sum_block),
-            dma((strips, 2)), dma((strips, 2)), dma((strips,)), dma((strips,)), dma((strips - 1,)), dma((strips - 1,)),
-            dma((2,)), dma((2,)), dma, dma, dma((max(steps, 1),)), dma((max(steps, 1),)), dma((2, 3)), dma((2, 3)),
+            *[dma((strips, CUTS, 2))] * 2, *[dma((strips, CUTS))] * 2, *[dma((strips - 1, CUTS))] * 2,
+            dma((2,)), dma((2,)), dma, dma, dma((max(steps, 1),)), dma((max(steps, 1),)), *[dma((1 + CUTS, 3))] * 2,
         ],
         compiler_params=pltpu.CompilerParams(
             collective_id=1, has_side_effects=True, vmem_limit_bytes=48 * MIB

time: 108 us -> 99.6 us (0.922)
  the two profiles are of different devices: /device:TPU:23 before, /device:TPU:0 now
where the time goes in v4:
time: 99.6 us; the launch traced here: 98.3 us
  Pallas kernels  89 us (89%)
  local copies, waits for them, and re-layouts  7.23 us (7%)
  between operations  1.31 us (1%)
    pallas_call x1, Pallas kernels, reduced(): pl.pallas_call(reduce_kernel, out_shape=(jax.ShapeDtypeStruct((planes - 1...  47.7 us
    pallas_call x1, Pallas kernels, halo(): pl.pallas_call(halo_kernel, out_shape=(jax.ShapeDtypeStruct((planes, stri...  23.1 us
    pallas_call x1, Pallas kernels, slots(): pl.pallas_call(slots_kernel, out_shape=(jax.ShapeDtypeStruct((planes + 1,...  18.3 us
    unnamed x12, local copies, waits for them, and re-layouts  7.15 us

profile of v4, /device:TPU:0, one launch (start us, length us, event | category | flops | bytes accessed | tf_op | source)
XLA Modules:
  0.0 98.3 jit_solution(14850248574311446112)
XLA Ops:
  1.3 0.1 pad.7.clone
  1.4 0.7 add_add_fusion
  2.1 0.0 copy-start
  2.1 1.2 %copy-done = f32[2,2,64,1024]{3,2,1,0:T(8,128)S(1)} copy-done((f32[2,2,64,1024]{3,2,1,0:T(8,128)S(1)}, f32[2,2,64,1024]{3,2,1,0:T(8,128)}, u32[]{:S(2)}) %copy-start) | copy-done | bytes 1048600
  3.3 0.0 copy-start.1
  3.3 1.0 %copy-done.1 = f32[1,1,8,128,128]{4,3,2,1,0:T(8,128)S(1)} copy-done((f32[1,1,8,128,128]{4,3,2,1,0:T(8,128)S(1)}, f32[1,1,8,128,128]{4,3,2,1,0:T(8,128)}, u32[]{:S(2)}) %copy-start.1) | copy-done | bytes 524312
  4.4 23.1 %halo.1 = (f32[4,192,1024]{2,1,0:T(8,128)S(1)}, s32[2,8,128]{2,1,0:T(8,128)S(1)}, f32[2,8,128,128]{3,2,1,0:T(8,128)S(1)}) custom-call(f32[4,64,1024]{2,1,0:T(8,128)S(1)} %bitcast.10, s32[8,128]{1,0:T(8,128)S(1)} %pad.4.info_ref, f32[8,128,128]{2,1,0:T(8,128)S(1)} %bitcast.12), custom_call_target="tpu_custom_call" | custom-call | tf_op jit(solution)/shard_map/halo/pallas_call | solution.py:344
  27.4 0.0 copy-start.2
  27.5 1.0 %copy-done.2 = f32[4,2,128,128]{3,2,1,0:T(8,128)S(1)} copy-done((f32[4,2,128,128]{3,2,1,0:T(8,128)S(1)}, f32[4,2,128,128]{3,2,1,0:T(8,128)}, u32[]{:S(2)}) %copy-start.2) | copy-done | bytes 524312
  28.5 0.0 copy-start.3
  28.5 1.0 %copy-done.3 = bf16[4,256,256]{2,1,0:T(8,128)(2,1)S(1)} copy-done((bf16[4,256,256]{2,1,0:T(8,128)(2,1)S(1)}, bf16[4,256,256]{2,1,0:T(8,128)(2,1)}, u32[]{:S(2)}) %copy-start.3) | copy-done | bytes 524312
  29.5 0.0 copy-start.4
  29.5 1.0 %copy-done.4 = bf16[4,256,256]{2,1,0:T(8,128)(2,1)S(1)} copy-done((bf16[4,256,256]{2,1,0:T(8,128)(2,1)S(1)}, bf16[4,256,256]{2,1,0:T(8,128)(2,1)}, u32[]{:S(2)}) %copy-start.4) | copy-done | bytes 524312
  30.6 18.3 %slots.1 = (f32[5,192,1024]{2,1,0:T(8,128)S(1)}, f32[9,128,128]{2,1,0:T(8,128)S(1)}) custom-call(s32[2,8,128]{2,1,0:T(8,128)S(1)} %get-tuple-element.9.info_ref, f32[4,192,1024]{2,1,0:T(8,128)S(1)} %get-tuple-element.10.object_ref, f32[4,2,128,128]{3,2,1,0:T(8,128)S(1)} %copy-done.2, f32[2,8,128,128]{3,2,1,0:T(8,128)S(1)} %get-tuple-element.11.measured_ref, ...), custom_call_target="tpu_custom_call" | custom-call | tf_op jit(solution)/shard_map/slots/pallas_call | solution.py:177
  48.9 47.7 %reduce.1 = (f32[4,64,1024]{2,1,0:T(8,128)S(1)}, f32[8,128,128]{2,1,0:T(8,128)S(1)}) custom-call(f32[5,192,1024]{2,1,0:T(8,128)S(1)} %get-tuple-element.12.stacked_ref, f32[9,128,128]{2,1,0:T(8,128)S(1)} %get-tuple-element.13.sums_ref), custom_call_target="tpu_custom_call" | custom-call | tf_op jit(solution)/shard_map/reduce/pallas_call | solution.py:530
  96.6 1.0 copy.13
  97.5 0.8 copy.14
  (1 shorter events, 0.0 us)
Async XLA Ops:
  2.1 1.2 %copy-start = (f32[2,2,64,1024]{3,2,1,0:T(8,128)S(1)}, f32[2,2,64,1024]{3,2,1,0:T(8,128)}, u32[]{:S(2)}) copy-start(f32[2,2,64,1024]{3,2,1,0:T(8,128)} %param.8) | copy-start | bytes 3145732
  3.3 1.0 %copy-start.1 = (f32[1,1,8,128,128]{4,3,2,1,0:T(8,128)S(1)}, f32[1,1,8,128,128]{4,3,2,1,0:T(8,128)}, u32[]{:S(2)}) copy-start(f32[1,1,8,128,128]{4,3,2,1,0:T(8,128)} %param.10) | copy-start | bytes 1572868
  27.4 1.0 %copy-start.2 = (f32[4,2,128,128]{3,2,1,0:T(8,128)S(1)}, f32[4,2,128,128]{3,2,1,0:T(8,128)}, u32[]{:S(2)}) copy-start(f32[4,2,128,128]{3,2,1,0:T(8,128)} %probe_ref.1) | copy-start | bytes 1572868
  28.5 1.0 %copy-start.3 = (bf16[4,256,256]{2,1,0:T(8,128)(2,1)S(1)}, bf16[4,256,256]{2,1,0:T(8,128)(2,1)}, u32[]{:S(2)}) copy-start(bf16[4,256,256]{2,1,0:T(8,128)(2,1)} %constant.7.clone.low_ref) | copy-start | bytes 1572868
  29.5 1.0 %copy-start.4 = (bf16[4,256,256]{2,1,0:T(8,128)(2,1)S(1)}, bf16[4,256,256]{2,1,0:T(8,128)(2,1)}, u32[]{:S(2)}) copy-start(bf16[4,256,256]{2,1,0:T(8,128)(2,1)} %constant.6.clone.high_ref) | copy-start | bytes 1572868
